TPU v7x, 32 devices: a whole 2x2x4 slice. The times are simulated.
32 devices in a mesh: tile: 8 (over z, x), depth: 4 (over y, core).
Axes of the slice: x: 2, y: 2, z: 4, core: 2. Of those that a mesh axis runs over, the one named last changes fastest.
Arguments:
- substrate_start: float32 [4, 2, 16, 16, 1024], P(None, None, 'depth', 'tile'), may hold values from -6 to 6
- adatom_start: float32 [40, 2, 24576], P(None, None, ('tile', 'depth')), may hold values from -6 to 6
- disorder: float32 [16, 16, 1024], P('depth', 'tile'), may hold values from -0.4 to 0.4
- adatom_block: float32 [40, 40], replicated, as said below
- coupling: float32 [4, 40], replicated, may hold values from -1 to 1
- adatom_tile: int32 [24576, 1], P(('tile', 'depth')), may hold values from 0 to 7; in each aligned block of 768 rows (0 to 767, 768 to 1535, ...) at most 192 rows name the same one
- adatom_spot: int32 [24576], P(('tile', 'depth')), may hold values from 0 to 2047
Outputs:
- substrate_prev: float32 [4, 2, 16, 16, 1024], P(None, None, 'depth', 'tile')
- substrate_last: float32 [4, 2, 16, 16, 1024], P(None, None, 'depth', 'tile')
- adatom_prev: float32 [40, 2, 24576], P(None, None, ('tile', 'depth'))
- adatom_last: float32 [40, 2, 24576], P(None, None, ('tile', 'depth'))
Inputs may be any that keep to these rules, and one draw needn't show every extreme that they name: `adatom_tile`: among the adatoms of one device, no tile is named by more than 192. adatom_block is symmetric.
All inputs are finite; a program needn't handle non-finite values.
Results may differ from a plain program's by a relative error of at most 0.0003.
Values sent between devices are 32-bit elements; how exact they have to be, the bound alone decides.
A program may use at most 64 MiB of HBM per device.

v0:
```python
import jax
import jax.numpy as jnp
from jax import lax
from jax.sharding import PartitionSpec as P

STEPS = 3


hopping = 0.12
chemical = 0.15
pairing = 0.3


def extended(shard, sides, width):
    for axis, dim in sides:
        size, length = (lax.axis_size(axis), shard.shape[dim])
        up = [(i, (i + 1) % size) for i in range(size - 1)]
        down = [(j, i) for i, j in up]
        last = lax.slice_in_dim(shard, length - width, length, axis=dim)
        first = lax.slice_in_dim(shard, 0, width, axis=dim)
        before = lax.ppermute(last, axis, up)
        after = lax.ppermute(first, axis, down)
        shard = jnp.concatenate([before, shard, after], axis=dim)
    return shard


def broadcast(shard, axis, root):
    mine = lax.axis_index(axis) == root
    return lax.psum(jnp.where(mine, shard, jnp.zeros_like(shard)), axis)


def substrate_terms(padded, field, disorder):
    beside = padded[:, :, 2:, 1:-1] + padded[:, :, :-2, 1:-1]
    beside = beside + padded[:, :, 1:-1, 2:] + padded[:, :, 1:-1, :-2]
    widened = jnp.pad(field, ((0, 0), (0, 0), (0, 0), (0, 0), (1, 1)))
    beside = beside + widened[..., 2:] + widened[..., :-2]
    signs = jnp.array([1.0, 1.0, -1.0, -1.0], jnp.float32).reshape(4, 1, 1, 1, 1)
    onsite = (disorder - chemical)[None, None] * field - hopping * beside
    partner = jnp.concatenate([field[2:], field[:2]], axis=0)
    return signs * onsite + pairing * partner


def per_device(
    substrate_start, adatom_start, disorder, adatom_block, coupling, adatom_tile, adatom_spot
):
    tiles = lax.axis_size("tile")
    count = adatom_spot.shape[0]
    capacity = 2 * count // tiles
    orbs, vecs, local_layers, rows, cols = substrate_start.shape
    width = orbs * vecs
    spots_n = rows * cols
    slots_n = tiles * capacity
    own_tile = adatom_tile[:, 0]
    onehot = (own_tile[:, None] == jnp.arange(tiles, dtype=jnp.int32)[None, :]).astype(jnp.bfloat16)
    lower = (
        lax.broadcasted_iota(jnp.int32, (count, count), 0)
        > lax.broadcasted_iota(jnp.int32, (count, count), 1)
    ).astype(jnp.bfloat16)
    before = jnp.dot(lower, onehot, preferred_element_type=jnp.float32)
    rank = jnp.sum(before * onehot.astype(jnp.float32), axis=1).astype(jnp.int32)
    slot = own_tile * capacity + rank
    sent_spots = (
        jnp.zeros((slots_n,), jnp.int32).at[slot].set(adatom_spot + 1).reshape(tiles, capacity)
    )
    got_spots = lax.all_to_all(sent_spots, "tile", split_axis=0, concat_axis=0, tiled=True).reshape(
        -1
    )
    row_index = jnp.maximum(got_spots - 1, 0)
    live = (got_spots > 0).astype(jnp.float32)
    on_top = lax.axis_index("depth") == 0

    def apply(sub, adatoms):
        padded = extended(sub, (("tile", 3), ("depth", 2)), 1)
        sub_out = substrate_terms(padded, sub, disorder)
        surface = sub[:, :, 0].reshape(width, spots_n)
        contrib = jnp.einsum(
            "oa,avn->nov", coupling, adatoms, precision=lax.Precision.HIGHEST
        ).reshape(count, width)
        sent = (
            jnp.zeros((slots_n, width), jnp.float32)
            .at[slot]
            .set(contrib)
            .reshape(tiles, capacity, width)
        )
        got = lax.all_to_all(sent, "tile", split_axis=0, concat_axis=0, tiled=True).reshape(
            slots_n, width
        )
        shared = broadcast(surface, "depth", 0)
        answer = jnp.take(shared, row_index, axis=1).T * live[:, None]
        local_add = jnp.zeros((spots_n, width), jnp.float32).at[row_index].add(got)
        added = lax.psum(local_add, "depth")
        back = lax.all_to_all(
            answer.reshape(tiles, capacity, width), "tile", split_axis=0, concat_axis=0, tiled=True
        ).reshape(slots_n, width)
        below = back[slot].T.reshape(orbs, vecs, count)
        ad_out = jnp.einsum("ab,bvn->avn", adatom_block, adatoms, precision=lax.Precision.HIGHEST)
        ad_out = ad_out + jnp.einsum(
            "oa,ovn->avn", coupling, below, precision=lax.Precision.HIGHEST
        )
        top_add = jnp.where(on_top, added, 0.0).T.reshape(orbs, vecs, rows, cols)
        sub_out = sub_out.at[:, :, 0].add(top_add)
        return (sub_out, ad_out)

    prev_sub, prev_ad = (substrate_start, adatom_start)
    cur_sub, cur_ad = apply(prev_sub, prev_ad)
    for step in range(STEPS - 1):
        new_sub, new_ad = apply(cur_sub, cur_ad)
        new_sub = 2.0 * new_sub - prev_sub
        new_ad = 2.0 * new_ad - prev_ad
        prev_sub, prev_ad = (cur_sub, cur_ad)
        cur_sub, cur_ad = (new_sub, new_ad)
    return (prev_sub, cur_sub, prev_ad, cur_ad)


def solution(mesh):
    in_specs = (
        P(None, None, "depth", "tile", None),
        P(None, None, ("tile", "depth")),
        P("depth", "tile", None),
        P(),
        P(),
        P(("tile", "depth"), None),
        P(("tile", "depth")),
    )
    out_specs = (
        P(None, None, "depth", "tile", None),
        P(None, None, "depth", "tile", None),
        P(None, None, ("tile", "depth")),
        P(None, None, ("tile", "depth")),
    )
    return jax.shard_map(
        per_device, mesh=mesh, in_specs=in_specs, out_specs=out_specs, check_vma=False
    )
```

profile of v0, /device:TPU:0, one launch (start us, length us, event | category | flops | bytes accessed | tf_op | source)
XLA Modules:
  0.0 343.2 jit_solution(13209028393839587191)
XLA Ops:
  9.7 3.4 scatter_custom_fusion
  13.8 7.3 %all-to-all-start = ((s32[8,1,192]{2,1,0:T(1,128)}), s32[8,1,192]{2,1,0:T(1,128)S(1)}, u32[]{:S(2)}, u32[]{:S(2)}) async-start(s32[8,1,192]{2,1,0:T(1,128)} %all_to_all.24), calls=%async_computation | async-start | bytes 16384 | tf_op jit(solution)/shard_map/all_to_all | solution.py:65
  22.3 3.9 %collective-permute-start = (f32[4,2,4,1,1024]{4,3,1,0,2:T(1,128)S(1)}, f32[4,2,4,1,1024]{4,3,1,0,2:T(1,128)S(1)}, u32[]{:S(2)}, u32[]{:S(2)}) collective-permute-start(f32[4,2,4,1,1024]{4,3,1,0,2:T(1,128)S(1)} %get-tuple-element.84), channel_id=1, source_target_pairs={{0,4},{4,8},{8,12},{12,16},{16,20},{20,24},{24,28},{1,5},{5,9},{9,... | collective-permute-start | bytes 393224 | tf_op jit(solution)/shard_map/ppermute | solution.py:21
  28.9 4.4 %scatter_custom_fusion.1 = f32[1536,8]{1,0:T(8,128)S(1)} fusion(s32[768]{0:T(1024)S(1)} %fusion.56, f32[768,8]{1,0:T(8,128)S(1)} %copy.140, f32[]{:T(128)} %constant.103.clone.1), kind=kCustom, calls=%fused_computation.46 | custom fusion | bytes 49156 | tf_op jit(solution)/shard_map/scatter | solution.py:82
  35.6 6.6 %all-to-all-start.1 = ((f32[8,192,8]{1,2,0:T(8,128)}), f32[8,192,8]{1,2,0:T(8,128)S(1)}, u32[]{:S(2)}, u32[]{:S(2)}) async-start(f32[8,192,8]{1,2,0:T(8,128)} %copy.141), calls=%async_computation.1 | async-start | bytes 131072 | tf_op jit(solution)/shard_map/all_to_all | solution.py:85
  42.5 6.6 %all-to-all-done.1 = f32[8,192,8]{1,2,0:T(8,128)S(1)} async-done(((f32[8,192,8]{1,2,0:T(8,128)}), f32[8,192,8]{1,2,0:T(8,128)S(1)}, u32[]{:S(2)}, u32[]{:S(2)}) %all-to-all-start.1) | async-done | bytes 49184 | tf_op jit(solution)/shard_map/all_to_all | solution.py:85
  49.3 10.7 %scatter_custom_fusion.2 = f32[2048,8]{1,0:T(8,128)} fusion(s32[1536]{0:T(1024)S(1)} %reshape.342, f32[1536,8]{1,0:T(8,128)S(1)} %bitcast.104, f32[]{:T(128)} %constant.103.clone.1), kind=kCustom, calls=%fused_computation.40 | custom fusion | flops 12288 | bytes 65540 | tf_op jit(solution)/shard_map/scatter-add | solution.py:90
  62.3 3.7 %collective-permute-start.3 = (f32[4,2,1,4,1024]{4,3,1,0,2:T(4,128)}, f32[4,2,1,4,1024]{4,3,1,0,2:T(4,128)}, u32[]{:S(2)}, u32[]{:S(2)}) collective-permute-start(f32[4,2,1,4,1024]{4,3,1,0,2:T(4,128)} %get-tuple-element.72), channel_id=1, source_target_pairs={{0,1},{1,2},{2,3},{4,5},{5,6},{6,7},{8,9},{9,10},{10,11},{12,13},{... | collective-permute-start | bytes 393224 | tf_op jit(solution)/shard_map/ppermute | solution.py:21
  66.0 44.2 %all-reduce.14.cloned.1.call-done = (f32[2048,8]{1,0:T(8,128)}, f32[8,2048]{0,1:T(8,128)}) async-done(((f32[2048,8]{1,0:T(8,128)}, f32[8,2048]{0,1:T(8,128)}), (f32[2048,8]{1,0:T(8,128)}, f32[8,2048]{0,1:T(8,128)})) %all-reduce.14.cloned.1.call-update) | async-done | bytes 131088 | tf_op jit(solution)/shard_map/psum | solution.py:91
  110.2 4.9 %gather_fusion.3 = f32[1536,8]{1,0:T(8,128)} fusion(f32[8,2048]{0,1:T(8,128)} %get-tuple-element.66, s32[2048]{0:T(1024)S(1)} %pad_clamp_fusion), kind=kCustom, calls=%fused_computation.clone | custom fusion | bytes 104448 | tf_op jit(solution)/shard_map/jit(_take)/gather | solution.py:89
  118.2 5.5 %all-to-all-start.2 = ((f32[8,192,8]{1,2,0:T(8,128)}), f32[8,192,8]{1,2,0:T(8,128)S(1)}, u32[]{:S(2)}, u32[]{:S(2)}) async-start(f32[8,192,8]{1,2,0:T(8,128)} %copy.148), calls=%async_computation.2 | async-start | bytes 131072 | tf_op jit(solution)/shard_map/all_to_all | solution.py:92
  124.2 6.4 %all-to-all-done.2 = f32[8,192,8]{1,2,0:T(8,128)S(1)} async-done(((f32[8,192,8]{1,2,0:T(8,128)}), f32[8,192,8]{1,2,0:T(8,128)S(1)}, u32[]{:S(2)}, u32[]{:S(2)}) %all-to-all-start.2) | async-done | bytes 49184 | tf_op jit(solution)/shard_map/all_to_all | solution.py:92
  133.9 4.4 %scatter_custom_fusion.3 = f32[1536,8]{1,0:T(8,128)S(1)} fusion(s32[768]{0:T(1024)S(1)} %fusion.56, f32[768,8]{1,0:T(8,128)S(1)} %copy.153, f32[]{:T(128)} %constant.103.clone.1), kind=kCustom, calls=%fused_computation.44 | custom fusion | bytes 49156 | tf_op jit(solution)/shard_map/scatter | solution.py:82
  139.2 3.3 all-to-all-start.3
  149.7 10.7 %scatter_custom_fusion.4 = f32[2048,8]{1,0:T(8,128)} fusion(s32[1536]{0:T(1024)S(1)} %reshape.342, f32[1536,8]{1,0:T(8,128)S(1)} %bitcast.105, f32[]{:T(128)} %constant.103.clone.1), kind=kCustom, calls=%fused_computation.38 | custom fusion | flops 12288 | bytes 65540 | tf_op jit(solution)/shard_map/scatter-add | solution.py:90
  165.0 44.8 %all-reduce.12.cloned.1.call-done = (f32[2048,8]{1,0:T(8,128)}, f32[8,2048]{0,1:T(8,128)}) async-done(((f32[2048,8]{1,0:T(8,128)}, f32[8,2048]{0,1:T(8,128)}), (f32[2048,8]{1,0:T(8,128)}, f32[8,2048]{0,1:T(8,128)})) %all-reduce.12.cloned.1.call-update) | async-done | bytes 131088 | tf_op jit(solution)/shard_map/psum | solution.py:91
  209.9 4.9 %gather_fusion.4 = f32[1536,8]{1,0:T(8,128)} fusion(f32[8,2048]{0,1:T(8,128)} %get-tuple-element.64, s32[2048]{0:T(1024)S(1)} %pad_clamp_fusion), kind=kCustom, calls=%fused_computation.1.clone | custom fusion | bytes 104448 | tf_op jit(solution)/shard_map/jit(_take)/gather | solution.py:89
  217.9 5.5 %all-to-all-start.4 = ((f32[8,192,8]{1,2,0:T(8,128)}), f32[8,192,8]{1,2,0:T(8,128)S(1)}, u32[]{:S(2)}, u32[]{:S(2)}) async-start(f32[8,192,8]{1,2,0:T(8,128)} %copy.160), calls=%async_computation.4 | async-start | bytes 131072 | tf_op jit(solution)/shard_map/all_to_all | solution.py:92
  234.3 4.4 %scatter_custom_fusion.5 = f32[1536,8]{1,0:T(8,128)S(1)} fusion(s32[768]{0:T(1024)S(1)} %fusion.56, f32[768,8]{1,0:T(8,128)S(1)} %copy.166, f32[]{:T(128)} %constant.103.clone.1), kind=kCustom, calls=%fused_computation.42 | custom fusion | bytes 49156 | tf_op jit(solution)/shard_map/scatter | solution.py:82
  239.6 5.1 %all-to-all-start.5 = ((f32[8,192,8]{1,2,0:T(8,128)}), f32[8,192,8]{1,2,0:T(8,128)S(1)}, u32[]{:S(2)}, u32[]{:S(2)}) async-start(f32[8,192,8]{1,2,0:T(8,128)} %copy.167), calls=%async_computation.5 | async-start | bytes 131072 | tf_op jit(solution)/shard_map/all_to_all | solution.py:85
  252.0 10.7 %scatter_custom_fusion.6 = f32[2048,8]{1,0:T(8,128)} fusion(s32[1536]{0:T(1024)S(1)} %reshape.342, f32[1536,8]{1,0:T(8,128)S(1)} %bitcast.103, f32[]{:T(128)} %constant.103.clone.1), kind=kCustom, calls=%fused_computation.36 | custom fusion | flops 12288 | bytes 65540 | tf_op jit(solution)/shard_map/scatter-add | solution.py:90
  267.4 45.2 %all-reduce.10.cloned.1.call-done = (f32[2048,8]{1,0:T(8,128)}, f32[8,2048]{0,1:T(8,128)}) async-done(((f32[2048,8]{1,0:T(8,128)}, f32[8,2048]{0,1:T(8,128)}), (f32[2048,8]{1,0:T(8,128)}, f32[8,2048]{0,1:T(8,128)})) %all-reduce.10.cloned.1.call-update) | async-done | bytes 131088 | tf_op jit(solution)/shard_map/psum | solution.py:91
  312.6 3.8 %gather_fusion.5 = f32[1536,8]{1,0:T(8,128)S(1)} fusion(f32[8,2048]{0,1:T(8,128)} %get-tuple-element.62, s32[2048]{0:T(1024)S(1)} %pad_clamp_fusion), kind=kCustom, calls=%fused_computation.2.clone | custom fusion | bytes 104448 | tf_op jit(solution)/shard_map/jit(_take)/gather | solution.py:89
  318.5 5.5 %all-to-all-start.6 = ((f32[8,192,8]{1,2,0:T(8,128)}), f32[8,192,8]{1,2,0:T(8,128)S(1)}, u32[]{:S(2)}, u32[]{:S(2)}) async-start(f32[8,192,8]{1,2,0:T(8,128)} %copy.172), calls=%async_computation.6 | async-start | bytes 131072 | tf_op jit(solution)/shard_map/all_to_all | solution.py:92
  (165 shorter events, 72.6 us)
Async XLA Ops:
  7.2 125.9 %copy-start = (f32[40,40]{1,0:T(8,128)S(1)}, f32[40,40]{1,0:T(8,128)}, u32[]{:S(2)}) copy-start(f32[40,40]{1,0:T(8,128)} %param.21) | copy-start | bytes 19204
  13.8 21.8 %all-to-all-start = ((s32[8,1,192]{2,1,0:T(1,128)}), s32[8,1,192]{2,1,0:T(1,128)S(1)}, u32[]{:S(2)}, u32[]{:S(2)}) async-start(s32[8,1,192]{2,1,0:T(1,128)} %all_to_all.24), calls=%async_computation | async-start | bytes 16384 | tf_op jit(solution)/shard_map/all_to_all | solution.py:65
  22.3 37.8 %collective-permute-start = (f32[4,2,4,1,1024]{4,3,1,0,2:T(1,128)S(1)}, f32[4,2,4,1,1024]{4,3,1,0,2:T(1,128)S(1)}, u32[]{:S(2)}, u32[]{:S(2)}) collective-permute-start(f32[4,2,4,1,1024]{4,3,1,0,2:T(1,128)S(1)} %get-tuple-element.84), channel_id=1, source_target_pairs={{0,4},{4,8},{8,12},{12,16},{16,20},{20,24},{24,28},{1,5},{5,9},{9,... | collective-permute-start | bytes 393224 | tf_op jit(solution)/shard_map/ppermute | solution.py:21
  26.3 33.8 %collective-permute-start.1 = (f32[4,2,4,1,1024]{4,3,1,0,2:T(1,128)S(1)}, f32[4,2,4,1,1024]{4,3,1,0,2:T(1,128)S(1)}, u32[]{:S(2)}, u32[]{:S(2)}) collective-permute-start(f32[4,2,4,1,1024]{4,3,1,0,2:T(1,128)S(1)} %get-tuple-element.83), channel_id=1, source_target_pairs={{4,0},{8,4},{12,8},{16,12},{20,16},{24,20},{28,24},{5,1},{9,5},{13... | collective-permute-start | bytes 393224 | tf_op jit(solution)/shard_map/ppermute | solution.py:22
  35.6 13.5 %all-to-all-start.1 = ((f32[8,192,8]{1,2,0:T(8,128)}), f32[8,192,8]{1,2,0:T(8,128)S(1)}, u32[]{:S(2)}, u32[]{:S(2)}) async-start(f32[8,192,8]{1,2,0:T(8,128)} %copy.141), calls=%async_computation.1 | async-start | bytes 131072 | tf_op jit(solution)/shard_map/all_to_all | solution.py:85
  42.2 68.0 %all-reduce.14.cloned.1.call-start = ((), (), s32[]{:S(2)}) async-start(), calls=%async_computation.9 | async-start | bytes 4194304 | tf_op jit(solution)/shard_map/psum | solution.py:91
  60.1 57.2 %copy-start.5 = (f32[4,2,4,1,1024]{4,3,1,0,2:T(1,128)}, f32[4,2,4,1,1024]{4,3,1,0,2:T(1,128)S(1)}, u32[]{:S(2)}) copy-start(f32[4,2,4,1,1024]{4,3,1,0,2:T(1,128)S(1)} %collective-permute-done) | copy-start | bytes 393220
  61.0 81.6 %collective-permute-start.2 = (f32[4,2,1,4,1024]{4,3,1,0,2:T(4,128)}, f32[4,2,1,4,1024]{4,3,1,0,2:T(4,128)}, u32[]{:S(2)}, u32[]{:S(2)}) collective-permute-start(f32[4,2,1,4,1024]{4,3,1,0,2:T(4,128)} %get-tuple-element.71), channel_id=1, source_target_pairs={{1,0},{2,1},{3,2},{5,4},{6,5},{7,6},{9,8},{10,9},{11,10},{13,12},{... | collective-permute-start | bytes 393224 | tf_op jit(solution)/shard_map/ppermute | solution.py:22
  62.3 80.3 %collective-permute-start.3 = (f32[4,2,1,4,1024]{4,3,1,0,2:T(4,128)}, f32[4,2,1,4,1024]{4,3,1,0,2:T(4,128)}, u32[]{:S(2)}, u32[]{:S(2)}) collective-permute-start(f32[4,2,1,4,1024]{4,3,1,0,2:T(4,128)} %get-tuple-element.72), channel_id=1, source_target_pairs={{0,1},{1,2},{2,3},{4,5},{5,6},{6,7},{8,9},{9,10},{10,11},{12,13},{... | collective-permute-start | bytes 393224 | tf_op jit(solution)/shard_map/ppermute | solution.py:21
  118.2 12.4 %all-to-all-start.2 = ((f32[8,192,8]{1,2,0:T(8,128)}), f32[8,192,8]{1,2,0:T(8,128)S(1)}, u32[]{:S(2)}, u32[]{:S(2)}) async-start(f32[8,192,8]{1,2,0:T(8,128)} %copy.148), calls=%async_computation.2 | async-start | bytes 131072 | tf_op jit(solution)/shard_map/all_to_all | solution.py:92
  139.2 10.2 %all-to-all-start.3 = ((f32[8,192,8]{1,2,0:T(8,128)}), f32[8,192,8]{1,2,0:T(8,128)S(1)}, u32[]{:S(2)}, u32[]{:S(2)}) async-start(f32[8,192,8]{1,2,0:T(8,128)} %copy.154), calls=%async_computation.3 | async-start | bytes 131072 | tf_op jit(solution)/shard_map/all_to_all | solution.py:85
  142.6 67.3 %all-reduce.12.cloned.1.call-start = ((), (), s32[]{:S(2)}) async-start(), calls=%async_computation.8 | async-start | bytes 4194304 | tf_op jit(solution)/shard_map/psum | solution.py:91
  160.4 63.4 %collective-permute-start.4 = (f32[4,2,4,1,1024]{4,3,1,0,2:T(1,128)}, f32[4,2,4,1,1024]{4,3,1,0,2:T(1,128)}, u32[]{:S(2)}, u32[]{:S(2)}) collective-permute-start(f32[4,2,4,1,1024]{4,3,1,0,2:T(1,128)} %get-tuple-element.80), channel_id=1, source_target_pairs={{0,4},{4,8},{8,12},{12,16},{16,20},{20,24},{24,28},{1,5},{5,9},{9,... | collective-permute-start | bytes 393224 | tf_op jit(solution)/shard_map/ppermute | solution.py:21
  163.8 60.1 %collective-permute-start.5 = (f32[4,2,4,1,1024]{4,3,1,0,2:T(1,128)}, f32[4,2,4,1,1024]{4,3,1,0,2:T(1,128)}, u32[]{:S(2)}, u32[]{:S(2)}) collective-permute-start(f32[4,2,4,1,1024]{4,3,1,0,2:T(1,128)} %get-tuple-element.79), channel_id=1, source_target_pairs={{4,0},{8,4},{12,8},{16,12},{20,16},{24,20},{28,24},{5,1},{9,5},{13... | collective-permute-start | bytes 393224 | tf_op jit(solution)/shard_map/ppermute | solution.py:22
  217.9 12.4 %all-to-all-start.4 = ((f32[8,192,8]{1,2,0:T(8,128)}), f32[8,192,8]{1,2,0:T(8,128)S(1)}, u32[]{:S(2)}, u32[]{:S(2)}) async-start(f32[8,192,8]{1,2,0:T(8,128)} %copy.160), calls=%async_computation.4 | async-start | bytes 131072 | tf_op jit(solution)/shard_map/all_to_all | solution.py:92
  224.9 20.0 %collective-permute-start.6 = (f32[4,2,1,4,1024]{4,3,1,0,2:T(4,128)S(1)}, f32[4,2,1,4,1024]{4,3,1,0,2:T(4,128)S(1)}, u32[]{:S(2)}, u32[]{:S(2)}) collective-permute-start(f32[4,2,1,4,1024]{4,3,1,0,2:T(4,128)S(1)} %get-tuple-element.69), channel_id=1, source_target_pairs={{1,0},{2,1},{3,2},{5,4},{6,5},{7,6},{9,8},{10,9},{11,10},{13,12},{... | collective-permute-start | bytes 393224 | tf_op jit(solution)/shard_map/ppermute | solution.py:22
  226.2 18.7 %collective-permute-start.7 = (f32[4,2,1,4,1024]{4,3,1,0,2:T(4,128)S(1)}, f32[4,2,1,4,1024]{4,3,1,0,2:T(4,128)S(1)}, u32[]{:S(2)}, u32[]{:S(2)}) collective-permute-start(f32[4,2,1,4,1024]{4,3,1,0,2:T(4,128)S(1)} %get-tuple-element.70), channel_id=1, source_target_pairs={{0,1},{1,2},{2,3},{4,5},{5,6},{6,7},{8,9},{9,10},{10,11},{12,13},{... | collective-permute-start | bytes 393224 | tf_op jit(solution)/shard_map/ppermute | solution.py:21
  239.6 12.0 %all-to-all-start.5 = ((f32[8,192,8]{1,2,0:T(8,128)}), f32[8,192,8]{1,2,0:T(8,128)S(1)}, u32[]{:S(2)}, u32[]{:S(2)}) async-start(f32[8,192,8]{1,2,0:T(8,128)} %copy.167), calls=%async_computation.5 | async-start | bytes 131072 | tf_op jit(solution)/shard_map/all_to_all | solution.py:85
  244.8 67.9 %all-reduce.10.cloned.1.call-start = ((), (), s32[]{:S(2)}) async-start(), calls=%async_computation.7 | async-start | bytes 4194304 | tf_op jit(solution)/shard_map/psum | solution.py:91
  263.4 62.2 %collective-permute-start.8 = (f32[4,2,4,1,1024]{4,3,1,0,2:T(1,128)}, f32[4,2,4,1,1024]{4,3,1,0,2:T(1,128)S(1)}, u32[]{:S(2)}, u32[]{:S(2)}) collective-permute-start(f32[4,2,4,1,1024]{4,3,1,0,2:T(1,128)} %get-tuple-element.76), channel_id=1, source_target_pairs={{0,4},{4,8},{8,12},{12,16},{16,20},{20,24},{24,28},{1,5},{5,9},{9,... | collective-permute-start | bytes 393224 | tf_op jit(solution)/shard_map/ppermute | solution.py:21
  266.1 59.6 %collective-permute-start.9 = (f32[4,2,4,1,1024]{4,3,1,0,2:T(1,128)}, f32[4,2,4,1,1024]{4,3,1,0,2:T(1,128)S(1)}, u32[]{:S(2)}, u32[]{:S(2)}) collective-permute-start(f32[4,2,4,1,1024]{4,3,1,0,2:T(1,128)} %get-tuple-element.75), channel_id=1, source_target_pairs={{4,0},{8,4},{12,8},{16,12},{20,16},{24,20},{28,24},{5,1},{9,5},{13... | collective-permute-start | bytes 393224 | tf_op jit(solution)/shard_map/ppermute | solution.py:22
  318.5 12.4 %all-to-all-start.6 = ((f32[8,192,8]{1,2,0:T(8,128)}), f32[8,192,8]{1,2,0:T(8,128)S(1)}, u32[]{:S(2)}, u32[]{:S(2)}) async-start(f32[8,192,8]{1,2,0:T(8,128)} %copy.172), calls=%async_computation.6 | async-start | bytes 131072 | tf_op jit(solution)/shard_map/all_to_all | solution.py:92
  325.9 8.6 %collective-permute-start.10 = (f32[4,2,1,4,1024]{4,3,1,0,2:T(4,128)S(1)}, f32[4,2,1,4,1024]{4,3,1,0,2:T(4,128)S(1)}, u32[]{:S(2)}, u32[]{:S(2)}) collective-permute-start(f32[4,2,1,4,1024]{4,3,1,0,2:T(4,128)S(1)} %get-tuple-element.67), channel_id=1, source_target_pairs={{1,0},{2,1},{3,2},{5,4},{6,5},{7,6},{9,8},{10,9},{11,10},{13,12},{... | collective-permute-start | bytes 393224 | tf_op jit(solution)/shard_map/ppermute | solution.py:22
  327.2 7.3 %collective-permute-start.11 = (f32[4,2,1,4,1024]{4,3,1,0,2:T(4,128)S(1)}, f32[4,2,1,4,1024]{4,3,1,0,2:T(4,128)S(1)}, u32[]{:S(2)}, u32[]{:S(2)}) collective-permute-start(f32[4,2,1,4,1024]{4,3,1,0,2:T(4,128)S(1)} %get-tuple-element.68), channel_id=1, source_target_pairs={{0,1},{1,2},{2,3},{4,5},{5,6},{6,7},{8,9},{9,10},{10,11},{12,13},{... | collective-permute-start | bytes 393224 | tf_op jit(solution)/shard_map/ppermute | solution.py:21
  (16 other events, 217.6 us)
Sparse Core Ops, SparseCore 0:
  60.2 49.9 all-reduce.13
  160.5 49.2 all-reduce.11
  262.8 49.7 all-reduce.9
where the time goes:
time: 345 us; the launch traced here: 343 us
  waiting for transfers between devices  153 us (44%)
  starting transfers between devices  66.9 us (19%)
  local copies, waits for them, and re-layouts  56 us (16%)
  other arithmetic  49.7 us (14%)
  between operations  14.6 us (4%)
    psum x3, waiting for transfers between devices, apply(): added = lax.psum(local_add, 'depth')  134 us
    scatter-add x3, other arithmetic, apply(): local_add = jnp.zeros((spots_n, width), jnp.float32).at[row_index].add(got)  32.1 us
    ppermute x6, starting transfers between devices, extended(): before = lax.ppermute(last, axis, up)  20.2 us
    all_to_all x3, starting transfers between devices, apply(): lax.all_to_all(answer.reshape(tiles, capacity, width), 'tile', split_axis...  16.5 us
    all_to_all x3, starting transfers between devices, apply(): lax.all_to_all(sent, 'tile', split_axis=0, concat_axis=0, tiled=True)  15.1 us
    gather x3, local copies, waits for them, and re-layouts, apply(): answer = jnp.take(shared, row_index, axis=1).T * live[:, None]  13.6 us
    scatter x3, local copies, waits for them, and re-layouts, apply(): sent = jnp.zeros((slots_n, width), jnp.float32).at[slot].set(contrib).res...  13.1 us
    all_to_all x3, waiting for transfers between devices, apply(): lax.all_to_all(sent, 'tile', split_axis=0, concat_axis=0, tiled=True)  10.6 us
  transfers between devices with their start and end apart: 22, of which 9 were waited for; matrix products, arithmetic and copies ran while one was open for 23% of the time, Pallas kernels for 0%

commit v1 on v0

v1 whole, which is shorter than its diff:
```python
import functools

import jax
import jax.numpy as jnp
from jax import lax
from jax.experimental import pallas as pl
from jax.experimental.pallas import tpu as pltpu
from jax.sharding import PartitionSpec as P

STEPS = 3
HOPPING = 0.12
CHEMICAL = 0.15
PAIRING = 0.3
ORB = 4
GROUP = 8
LIVE, HIGH, LOW = 12, 13, 14

MESH = pl.DeviceIdType.MESH
HIGHEST = lax.Precision.HIGHEST
NN = (((1,), (0,)), ((), ()))
NT = (((1,), (1,)), ((), ()))


def each(count, body):
    if count <= GROUP:
        for i in range(count):
            body(i)
    else:

        def run(i, carry):
            body(i)
            return carry

        lax.fori_loop(0, count, run, 0)


def exact(a, b, dims=NN):
    return lax.dot_general(a, b, dims, precision=HIGHEST, preferred_element_type=jnp.float32)


def product(a, b, dims=NN):
    return lax.dot_general(a, b, dims, preferred_element_type=jnp.float32)


def halves(x):
    first = x.astype(jnp.bfloat16).astype(jnp.float32)
    return first, (x - first).astype(jnp.bfloat16).astype(jnp.float32)


def iota(shape, dim):
    return lax.broadcasted_iota(jnp.int32, shape, dim)


def kernel(
    tiles, depths,
    s0, adatoms, disorder, block, coupling, tile_of, spot_of,
    s2, s3, a2, a3,
    s1, hx, hl, top, send, got, lhs, low_t, high, scat, red_a, red_b, ans, back, proj, rank_t, a1,
    hx_s, hx_r, hl_s, hl_r, top_s, top_r, go_s, go_r, ra_s, ra_r, rb_s, rb_r, an_s, an_r,
):
    t = lax.axis_index("tile")
    d = lax.axis_index("depth")
    rows, layers, fields = s0.shape[:3]
    count = tile_of.shape[1]
    slots = send.shape[2]
    lines = rows * 8
    states = [s0, s1, s2, s3]

    barrier = pltpu.get_barrier_semaphore()

    def greet_tile(i):
        pl.semaphore_signal(
            barrier, inc=1, device_id=(lax.rem(t + i + 1, tiles), d), device_id_type=MESH
        )

    def greet_depth(i):
        pl.semaphore_signal(
            barrier, inc=1, device_id=(t, lax.rem(d + i + 1, depths)), device_id_type=MESH
        )

    each(tiles - 1, greet_tile)
    each(depths - 1, greet_depth)

    for side, (edge_t, edge_d) in enumerate(((0, 0), (tiles - 1, depths - 1))):

        @pl.when(t == edge_t)
        def _():
            hx[:, side] = jnp.zeros_like(hx[:, side])

        @pl.when(d == edge_d)
        def _():
            hl[:, side] = jnp.zeros_like(hl[:, side])

    pl.semaphore_wait(barrier, tiles - 1 + depths - 1)

    def halo(k, side):
        state = states[k]
        step = 1 if side == 0 else -1
        row = rows - 1 if side == 0 else 0
        layer = layers - 1 if side == 0 else 0
        along_x = pltpu.make_async_remote_copy(
            src_ref=state.at[row], dst_ref=hx.at[k, side],
            send_sem=hx_s.at[k, side], recv_sem=hx_r.at[k, side],
            device_id=(lax.rem(t + step + tiles, tiles), d), device_id_type=MESH,
        )
        along_l = pltpu.make_async_remote_copy(
            src_ref=state.at[:, layer], dst_ref=hl.at[k, side],
            send_sem=hl_s.at[k, side], recv_sem=hl_r.at[k, side],
            device_id=(t, lax.rem(d + step + depths, depths)), device_id_type=MESH,
        )
        return along_x, along_l

    def sends(side):
        if side == 0:
            return t < tiles - 1, d < depths - 1
        return t > 0, d > 0

    def takes(side):
        if side == 0:
            return t > 0, d > 0
        return t < tiles - 1, d < depths - 1

    def halo_start(k):
        for side in range(2):
            for copy, there in zip(halo(k, side), sends(side)):
                pl.when(there)(copy.start)

    def halo_wait(k):
        for side in range(2):
            for copy, there in zip(halo(k, side), takes(side)):
                pl.when(there)(copy.wait_recv)

    def halo_sent(k):
        for side in range(2):
            for copy, there in zip(halo(k, side), sends(side)):
                pl.when(there)(copy.wait_send)

    def top_copy(k, i):
        return pltpu.make_async_remote_copy(
            src_ref=top.at[k], dst_ref=top.at[k],
            send_sem=top_s.at[k, i], recv_sem=top_r.at[k],
            device_id=(t, i + 1), device_id_type=MESH,
        )

    def top_start(k):
        @pl.when(d == 0)
        def _():
            top[k] = states[k][:, 0]
            each(depths - 1, lambda i: top_copy(k, i).start())

    def top_wait(k):
        pl.when(d > 0)(lambda: top_copy(k, 0).wait_recv())

    def peer(i):
        return lax.rem(t + i + 1, tiles)

    def go_copy(other, to):
        return pltpu.make_async_remote_copy(
            src_ref=send.at[other], dst_ref=got.at[to],
            send_sem=go_s.at[other], recv_sem=go_r.at[to],
            device_id=(other, d), device_id_type=MESH,
        )

    def answer_copy(k, other, to):
        return pltpu.make_async_remote_copy(
            src_ref=ans.at[k, other], dst_ref=back.at[k, to],
            send_sem=an_s.at[k, other], recv_sem=an_r.at[k, to],
            device_id=(other, d), device_id_type=MESH,
        )

    def partial_copy(part, i):
        if part == 0:
            src, dst, ss, rs = scat.at[pl.ds(0, 8)], red_a, ra_s, ra_r
        else:
            src, dst, ss, rs = scat.at[pl.ds(8, 17)], red_b, rb_s, rb_r
        return pltpu.make_async_remote_copy(
            src_ref=src, dst_ref=dst.at[i], send_sem=ss, recv_sem=rs.at[i],
            device_id=(t, 0), device_id_type=MESH,
        )

    def reduce_wait(part):
        first, length = ((0, 8), (8, 17))[part]
        buffer = (red_a, red_b)[part]

        def add(i):
            partial_copy(part, i).wait_recv()
            scat[pl.ds(first, length)] += buffer[i]

        each(depths - 1, add)

    lane = iota((8, 8, 128), 2)
    sub = iota((8, 8, 128), 1)
    plus = iota((8, 8, 128), 0) % ORB < 2

    def stencil(k):
        field, out = states[k], states[k + 1]
        for x in range(rows):
            for l in range(layers):
                f = field[x, l]
                beside = field[x, l - 1] if l > 0 else hl[k, 0, x]
                beside += field[x, l + 1] if l < layers - 1 else hl[k, 1, x]
                beside += field[x - 1, l] if x > 0 else hx[k, 0, l]
                beside += field[x + 1, l] if x < rows - 1 else hx[k, 1, l]
                r = pltpu.roll(f, 1, 2)
                c = jnp.where(sub == 0, 0.0, pltpu.roll(r, 1, 1))
                beside += jnp.where(lane == 0, c, r)
                r = pltpu.roll(f, 127, 2)
                c = jnp.where(sub == 7, 0.0, pltpu.roll(r, 7, 1))
                beside += jnp.where(lane == 127, c, r)
                onsite = (disorder[x, l] - CHEMICAL)[None] * f - HOPPING * beside
                partner = jnp.concatenate([f[2:4], f[0:2], f[6:8], f[4:6]], axis=0)
                new = jnp.where(plus, onsite, -onsite) + PAIRING * partner
                if k > 0:
                    new = 2.0 * new - states[k - 1][x, l]
                out[x, l] = new

    halo_start(0)
    top_start(0)

    b, c = block[...], coupling[...]
    cb = exact(c, b)
    proj[0:4] = c
    proj[4:8] = cb
    proj[8:12] = exact(cb, b)
    proj[12:16] = jnp.zeros((4, b.shape[0]), jnp.float32)
    pair1 = exact(c, c, NT)
    pair2 = exact(cb, c, NT)
    values = exact(proj[...], adatoms[...])
    values = jnp.concatenate([values[:, :count], values[:, count:]], axis=0)
    spot = spot_of[...]
    row = iota(values.shape, 0)
    values = jnp.where(row == LIVE, 1.0, values)
    values = jnp.where(row == HIGH, (spot // 128).astype(jnp.float32), values)
    values = jnp.where(row == LOW, (spot % 128).astype(jnp.float32), values)
    owner = (iota((tiles, count), 0) == tile_of[...]).astype(jnp.float32)
    earlier = (iota((count, count), 0) < iota((count, count), 1)).astype(jnp.float32)
    before = product(owner.astype(jnp.bfloat16), earlier.astype(jnp.bfloat16))
    rank = jnp.sum(owner * before, axis=0, keepdims=True).astype(jnp.int32)
    rank_t[...] = (iota((slots, count), 0) == rank).astype(jnp.float32).astype(jnp.bfloat16)
    parts = jnp.concatenate(halves(values), axis=0)

    def compact(g):
        chosen = [
            jnp.where(tile_of[...] == g * GROUP + i, parts, 0.0).astype(jnp.bfloat16)
            for i in range(GROUP)
        ]
        packed = product(jnp.concatenate(chosen, axis=0), rank_t[...], NT)
        for i in range(GROUP):
            at = i * 64
            send[g * GROUP + i] = packed[at : at + 32] + packed[at + 32 : at + 64]

    each(tiles // GROUP, compact)
    each(tiles - 1, lambda i: go_copy(peer(i), t).start())
    got[t] = send[t]

    halo_wait(0)
    stencil(0)

    each(tiles - 1, lambda i: go_copy(peer(i), peer(i)).wait_recv())

    order = [v * 16 + j * 4 + o for j in range(STEPS) for v in range(2) for o in range(ORB)]
    order.append(LIVE)
    terms = len(order)

    def scatter(g):
        for i in range(GROUP):
            u = g * GROUP + i
            data = got[u]
            first, second = halves(data)
            here = iota((lines, slots), 0).astype(jnp.float32) == data[HIGH : HIGH + 1]
            high[u] = here.astype(jnp.float32)
            low = iota((128, slots), 0).astype(jnp.float32) == data[LOW : LOW + 1]
            low_t[u] = low.astype(jnp.float32).astype(jnp.bfloat16)
            for at, q in enumerate(order):
                for p, part in enumerate((first, second)):
                    if q == LIVE and p == 1:
                        continue
                    line = (p * terms + at) * lines
                    lhs[line : line + lines, i * slots : (i + 1) * slots] = jnp.where(
                        here, part[q : q + 1], 0.0
                    ).astype(jnp.bfloat16)
        total = jnp.zeros((lhs.shape[0], 128), jnp.float32)
        for i in range(GROUP):
            total += product(
                lhs[:, i * slots : (i + 1) * slots], low_t[g * GROUP + i], NT
            )
        half = terms * lines
        merged = total[: half - lines] + total[half:]
        merged = merged.reshape(terms - 1, rows, 8, 128)
        counted = total[half - lines : half].reshape(rows, 8, 128)
        if tiles == GROUP:
            scat[0 : terms - 1] = merged
            scat[terms - 1] = counted
        else:
            scat[0 : terms - 1] += merged
            scat[terms - 1] += counted

    if tiles > GROUP:
        scat[...] = jnp.zeros_like(scat)
    each(tiles // GROUP, scatter)

    @pl.when(d > 0)
    def _():
        partial_copy(0, d - 1).start()
        partial_copy(1, d - 1).start()

    @pl.when(d == 0)
    def _():
        reduce_wait(0)
        for x in range(rows):
            s1[x, 0] += scat[0:8, x]

    halo_start(1)
    top_start(1)

    def gather(k):
        top_wait(k)
        first, second = halves(top[k].reshape(rows * 8 * 8, 128))
        both = jnp.concatenate([first, second], axis=0).astype(jnp.bfloat16)

        def one(u):
            found = product(both, low_t[u])
            half = rows * 64
            found = (found[:half] + found[half:]).reshape(rows, 8, 8, slots)
            found = found * high[u].reshape(rows, 1, 8, slots)
            ans[k, u] = jnp.sum(jnp.sum(found, axis=0), axis=1)

        each(tiles, one)
        each(tiles - 1, lambda i: answer_copy(k, peer(i), t).start())
        back[k, t] = ans[k, t]

    def below(k):
        each(tiles - 1, lambda i: answer_copy(k, peer(i), peer(i)).wait_recv())
        first, second = halves(back[k].reshape(tiles * 8, slots))
        both = jnp.concatenate([first, second], axis=0).astype(jnp.bfloat16)
        found = product(both, rank_t[...])
        found = (found[: tiles * 8] + found[tiles * 8 :]).reshape(tiles, 8, count)
        found = jnp.sum(found * owner.reshape(tiles, 1, count), axis=0)
        return jnp.concatenate([found[0:4], found[4:8]], axis=1)

    ct = exact((iota(b.shape, 0) == iota(b.shape, 1)).astype(jnp.float32), c, NT)

    def adatom_part(k, vector):
        return exact(b, vector) + exact(ct, below(k))

    def mixed(pair, state, x):
        sums = []
        for v in range(2):
            for o in range(ORB):
                total = None
                for m in range(ORB):
                    term = pair[o : o + 1, m : m + 1] * state[x, 0, v * ORB + m]
                    total = term if total is None else total + term
                sums.append(total[None])
        return jnp.concatenate(sums, axis=0)

    gather(0)
    halo_wait(1)
    stencil(1)

    @pl.when(d == 0)
    def _():
        reduce_wait(1)
        for x in range(rows):
            extra = scat[8:16, x] + scat[24, x][None] * mixed(pair1, s0, x)
            s2[x, 0] += 2.0 * extra

    halo_start(2)
    top_start(2)
    gather(1)
    a1[...] = adatom_part(0, adatoms[...])
    gather(2)
    halo_wait(2)
    stencil(2)

    @pl.when(d == 0)
    def _():
        for x in range(rows):
            pairs = mixed(pair2, s0, x) + mixed(pair1, s1, x)
            extra = scat[16:24, x] + scat[24, x][None] * pairs
            s3[x, 0] += 2.0 * (2.0 * extra - scat[0:8, x])

    a2[...] = 2.0 * adatom_part(1, a1[...]) - adatoms[...]
    a3[...] = 2.0 * adatom_part(2, a2[...]) - a1[...]

    each(tiles - 1, lambda i: go_copy(peer(i), t).wait_send())
    for k in range(STEPS):
        halo_sent(k)
        each(tiles - 1, lambda i: answer_copy(k, peer(i), t).wait_send())

    @pl.when(d == 0)
    def _():
        for k in range(STEPS):
            each(depths - 1, lambda i: top_copy(k, i).wait_send())

    @pl.when(d > 0)
    def _():
        partial_copy(0, d - 1).wait_send()
        partial_copy(1, d - 1).wait_send()


def per_device(
    substrate_start, adatom_start, disorder, adatom_block, coupling, adatom_tile, adatom_spot
):
    tiles, depths = lax.axis_size("tile"), lax.axis_size("depth")
    count = adatom_spot.shape[0]
    orbs, vecs, layers, rows, cols = substrate_start.shape
    orba = adatom_block.shape[0]
    capacity = 2 * count // tiles
    slots = -(-capacity // 128) * 128
    sites = substrate_start.reshape(orbs, vecs, layers, rows, 8, 128)
    sites = sites.transpose(3, 2, 1, 0, 4, 5).reshape(rows, layers, 8, 8, 128)
    potential = disorder.reshape(layers, rows, 8, 128).transpose(1, 0, 2, 3)
    vectors = adatom_start.reshape(orba, vecs * count)
    f32 = jnp.float32
    state = jax.ShapeDtypeStruct(sites.shape, f32)
    flat = jax.ShapeDtypeStruct(vectors.shape, f32)
    lines = rows * 8
    dma = pltpu.SemaphoreType.DMA
    vmem = pl.BlockSpec(memory_space=pltpu.VMEM)
    s2, s3, a2, a3 = pl.pallas_call(
        functools.partial(kernel, tiles, depths),
        out_shape=(state, state, flat, flat),
        in_specs=[vmem] * 7,
        out_specs=(vmem,) * 4,
        scratch_shapes=[
            pltpu.VMEM(sites.shape, f32),
            pltpu.VMEM((STEPS, 2, layers, 8, 8, 128), f32),
            pltpu.VMEM((STEPS, 2, rows, 8, 8, 128), f32),
            pltpu.VMEM((STEPS, rows, 8, 8, 128), f32),
            pltpu.VMEM((tiles, 32, slots), f32),
            pltpu.VMEM((tiles, 32, slots), f32),
            pltpu.VMEM((49 * lines, GROUP * slots), jnp.bfloat16),
            pltpu.VMEM((tiles, 128, slots), jnp.bfloat16),
            pltpu.VMEM((tiles, lines, slots), f32),
            pltpu.VMEM((25, rows, 8, 128), f32),
            pltpu.VMEM((depths - 1, 8, rows, 8, 128), f32),
            pltpu.VMEM((depths - 1, 17, rows, 8, 128), f32),
            pltpu.VMEM((STEPS, tiles, 8, slots), f32),
            pltpu.VMEM((STEPS, tiles, 8, slots), f32),
            pltpu.VMEM((16, orba), f32),
            pltpu.VMEM((slots, count), jnp.bfloat16),
            pltpu.VMEM(vectors.shape, f32),
            dma((STEPS, 2)), dma((STEPS, 2)), dma((STEPS, 2)), dma((STEPS, 2)),
            dma((STEPS, depths - 1)), dma((STEPS,)),
            dma((tiles,)), dma((tiles,)),
            dma, dma((depths - 1,)), dma, dma((depths - 1,)),
            dma((STEPS, tiles)), dma((STEPS, tiles)),
        ],
        compiler_params=pltpu.CompilerParams(
            collective_id=0, has_side_effects=True, vmem_limit_bytes=56 * 1024 * 1024
        ),
    )(
        sites, vectors, potential, adatom_block, coupling,
        adatom_tile.reshape(1, count), adatom_spot.reshape(1, count),
    )

    def unpack(s):
        s = s.reshape(rows, layers, vecs, orbs, 8, 128).transpose(3, 2, 1, 0, 4, 5)
        return s.reshape(substrate_start.shape)

    return unpack(s2), unpack(s3), a2.reshape(adatom_start.shape), a3.reshape(adatom_start.shape)


def solution(mesh):
    in_specs = (
        P(None, None, "depth", "tile", None),
        P(None, None, ("tile", "depth")),
        P("depth", "tile", None),
        P(),
        P(),
        P(("tile", "depth"), None),
        P(("tile", "depth")),
    )
    out_specs = (
        P(None, None, "depth", "tile", None),
        P(None, None, "depth", "tile", None),
        P(None, None, ("tile", "depth")),
        P(None, None, ("tile", "depth")),
    )
    return jax.shard_map(
        per_device, mesh=mesh, in_specs=in_specs, out_specs=out_specs, check_vma=False
    )
```

time: 345 us -> 50.3 us (0.15)
  waiting for transfers between devices: 153 us -> 0 us
  starting transfers between devices: 66.9 us -> 0 us
  other arithmetic: 49.7 us -> 0 us
  local copies, waits for them, and re-layouts: 56 us -> 10.1 us
  Pallas kernels: 0 us -> 39.2 us
  between operations: 14.6 us -> 0.67 us
    psum x3 -> x0, waiting for transfers between devices: 134 us -> none  [apply(): added = lax.psum(local_add, 'depth')]
    pallas_call x0 -> x1, Pallas kernels: none -> 39.2 us  [per_device(): pl.pallas_call(functools.partial(kernel, tiles, depths), out_shape=(state...]
    all_to_all x7 -> x0, starting transfers between devices: 38.9 us -> none  [the longest x3 16.5 us: apply(): lax.all_to_all(answer.reshape(tiles, capacity, width), 'tile', split_axis...]
    scatter-add x5 -> x0, other arithmetic: 32.2 us -> none  [the longest x3 32.1 us: apply(): local_add = jnp.zeros((spots_n, width), jnp.float32).at[row_index].add(got)]
    ppermute x12 -> x0, starting transfers between devices: 27.9 us -> none  [the longest x6 20.2 us: extended(): before = lax.ppermute(last, axis, up)]
    all_to_all x7 -> x0, waiting for transfers between devices: 18.3 us -> none  [the longest x3 10.6 us: apply(): lax.all_to_all(sent, 'tile', split_axis=0, concat_axis=0, tiled=True)]
    gather x6 -> x0, local copies, waits for them, and re-layouts: 18.3 us -> none  [the longest x3 13.6 us: apply(): answer = jnp.take(shared, row_index, axis=1).T * live[:, None]]
    scatter x4 -> x0, local copies, waits for them, and re-layouts: 16.5 us -> none  [the longest x3 13.1 us: apply(): sent = jnp.zeros((slots_n, width), jnp.float32).at[slot].set(contrib).res...]
  transfers between devices with their start and end apart: 22 -> 0, of which waited for: 9 -> 0; matrix products, arithmetic and copies ran while one was open for 23% -> 0% of each run, Pallas kernels for 0% -> 0%
where the time goes in v1:
time: 50.3 us; the launch traced here: 49.9 us
  Pallas kernels  39.2 us (78%)
  local copies, waits for them, and re-layouts  10.1 us (20%)
  between operations  0.67 us (1%)
    pallas_call x1, Pallas kernels, per_device(): pl.pallas_call(functools.partial(kernel, tiles, depths), out_shape=(state...  39.2 us
    reshape x4, local copies, waits for them, and re-layouts, unpack(): return s.reshape(substrate_start.shape)  2.94 us
    unnamed x9, local copies, waits for them, and re-layouts  1.85 us
    reshape x2, local copies, waits for them, and re-layouts, per_device(): potential = disorder.reshape(layers, rows, 8, 128).transpose(1, 0, 2, 3)  1.4 us
    reshape x1, local copies, waits for them, and re-layouts, per_device(): adatom_spot.reshape(1, count)  1.27 us

profile of v1, /device:TPU:0, one launch (start us, length us, event | category | flops | bytes accessed | tf_op | source)
XLA Modules:
  0.0 49.9 jit_solution(8103528012173618744)
XLA Ops:
  0.6 1.3 %reshape.49.spot_of = s32[1,768]{1,0:T(1,128)} reshape(s32[768]{0:T(1024)} %param.13) | data formatting | bytes 6144 | tf_op jit(solution)/shard_map/reshape | solution.py:455
  1.9 0.8 %reshape.56 = f32[4,2,8,128]{3,2,1,0:T(8,128)S(1)} reshape(f32[4,2,1024]{2,1,0:T(2,128)} %param.9) | data formatting | bytes 65536 | tf_op jit(solution)/shard_map/reshape | solution.py:413
  2.7 0.6 %copy.20 = f32[4,2,8,128]{3,2,0,1:T(8,128)} copy(f32[4,2,8,128]{3,2,1,0:T(8,128)S(1)} %reshape.56) | data formatting | bytes 65536 | tf_op jit(solution)/shard_map/reshape | solution.py:413
  3.3 0.0 copy-start
  3.3 1.7 %copy.18 = f32[5,8,2,768]{3,1,2,0:T(8,128)} copy(f32[5,8,2,768]{3,2,1,0:T(2,128)} %bitcast.27) | data formatting | bytes 491520
  5.0 0.0 copy-done
  5.0 0.2 reshape.44
  5.2 0.7 %copy.11 = f32[4,2,4,2,8,128]{5,4,0,1,2,3:T(8,128)} copy(f32[4,2,4,2,8,128]{5,4,3,2,1,0:T(8,128)S(1)} %reshape.44) | data formatting | bytes 524288 | tf_op jit(solution)/shard_map/reshape | solution.py:411
  5.9 39.2 %shard_map.102 = (f32[2,4,8,8,128]{4,3,2,1,0:T(8,128)}, f32[2,4,8,8,128]{4,3,2,1,0:T(8,128)}, f32[40,1536]{1,0:T(8,128)}, f32[40,1536]{1,0:T(8,128)}) custom-call(f32[2,4,8,8,128]{4,3,2,1,0:T(8,128)} %bitcast.23, f32[40,1536]{1,0:T(8,128)} %bitcast.24, f32[2,4,8,128]{3,2,1,0:T(8,128)} %bitcast.28, f32[40,40]{1,0:T(8,128)} %block.1, f32[4,40]{1,0:T(4,128)} %coupling.1, ...), custom_call_target="tpu_custom_call" | custom-call | tf_op jit(solution)/shard_map/pallas_call | solution.py:421
  45.1 1.0 %reshape.57 = f32[4,2,4,2,1024]{4,0,1,2,3:T(4,128)S(1)} reshape(f32[4,2,4,2,8,128]{5,4,0,1,2,3:T(8,128)} %bitcast.26) | data formatting | bytes 524288 | tf_op jit(solution)/shard_map/reshape | solution.py:460
  46.1 0.0 copy-start.1
  46.2 0.9 %copy.16 = f32[4,2,4,2,1024]{4,3,2,1,0:T(2,128)} copy(f32[4,2,4,2,1024]{4,0,1,2,3:T(4,128)S(1)} %reshape.57) | data formatting | bytes 524288 | tf_op jit(solution)/shard_map/reshape | solution.py:460
  47.1 0.0 copy-done.1
  47.1 0.1 reshape.58
  47.2 0.0 copy-start.3
  47.2 0.9 %copy.17 = f32[4,2,4,2,1024]{4,3,2,1,0:T(2,128)} copy(f32[4,2,4,2,1024]{4,0,1,2,3:T(4,128)S(1)} %reshape.58) | data formatting | bytes 524288 | tf_op jit(solution)/shard_map/reshape | solution.py:460
  48.1 0.0 copy-done.3
  48.1 0.0 copy-start.2
  48.1 0.9 %reshape.54 = f32[40,2,768]{2,1,0:T(2,128)} reshape(f32[40,1536]{1,0:T(8,128)S(1)} %copy-done.3) | data formatting | bytes 491520 | tf_op jit(solution)/shard_map/reshape | solution.py:462
  49.0 0.1 copy-done.2
  49.1 0.9 %reshape.55 = f32[40,2,768]{2,1,0:T(2,128)} reshape(f32[40,1536]{1,0:T(8,128)S(1)} %copy-done.2) | data formatting | bytes 491520 | tf_op jit(solution)/shard_map/reshape | solution.py:462
Async XLA Ops:
  3.3 1.7 %copy-start = (f32[4,2,4,2,1024]{4,3,2,1,0:T(2,128)S(1)}, f32[4,2,4,2,1024]{4,3,2,1,0:T(2,128)}, u32[]{:S(2)}) copy-start(f32[4,2,4,2,1024]{4,3,2,1,0:T(2,128)} %param.7) | copy-start | bytes 786436
  46.1 1.0 %copy-start.1 = (f32[2,4,8,8,128]{4,3,2,1,0:T(8,128)S(1)}, f32[2,4,8,8,128]{4,3,2,1,0:T(8,128)}, u32[]{:S(2)}) copy-start(f32[2,4,8,8,128]{4,3,2,1,0:T(8,128)} %get-tuple-element.9) | copy-start | bytes 786436
  47.2 0.9 %copy-start.3 = (f32[40,1536]{1,0:T(8,128)S(1)}, f32[40,1536]{1,0:T(8,128)}, u32[]{:S(2)}) copy-start(f32[40,1536]{1,0:T(8,128)} %get-tuple-element.10) | copy-start | bytes 737284
  48.1 0.9 %copy-start.2 = (f32[40,1536]{1,0:T(8,128)S(1)}, f32[40,1536]{1,0:T(8,128)}, u32[]{:S(2)}) copy-start(f32[40,1536]{1,0:T(8,128)} %get-tuple-element.11) | copy-start | bytes 737284

commit v2 on v1

--- a/solution.py
+++ b/solution.py
@@ -53,18 +53,23 @@
 
 def kernel(
     tiles, depths,
-    s0, adatoms, disorder, block, coupling, tile_of, spot_of,
-    s2, s3, a2, a3,
-    s1, hx, hl, top, send, got, lhs, low_t, high, scat, red_a, red_b, ans, back, proj, rank_t, a1,
+    sub_in, ad_in, dis_in, block, coupling, tile_of, spot_of,
+    sub_prev, sub_last, ad_prev, ad_last,
+    s0, s1, s2, s3, adatoms, disorder,
+    hx, hl, top, send, got, lhs, low_t, high, scat, red_a, red_b, ans, back, proj, rank_t, a1, a2,
     hx_s, hx_r, hl_s, hl_r, top_s, top_r, go_s, go_r, ra_s, ra_r, rb_s, rb_r, an_s, an_r,
 ):
     t = lax.axis_index("tile")
     d = lax.axis_index("depth")
-    rows, layers, fields = s0.shape[:3]
+    rows, layers = s0.shape[:2]
     count = tile_of.shape[1]
     slots = send.shape[2]
-    lines = rows * 8
+    sites = rows * 128
     states = [s0, s1, s2, s3]
+    order_l = list(range(layers // 2, layers)) + list(range(layers // 2 - 1, -1, -1))
+
+    def spread(x):
+        return pl.ds(x, 8, stride=rows)
 
     barrier = pltpu.get_barrier_semaphore()
 
@@ -91,49 +96,50 @@
         def _():
             hl[:, side] = jnp.zeros_like(hl[:, side])
 
-    pl.semaphore_wait(barrier, tiles - 1 + depths - 1)
-
-    def halo(k, side):
-        state = states[k]
+    def along_x(k, side, layer):
         step = 1 if side == 0 else -1
-        row = rows - 1 if side == 0 else 0
-        layer = layers - 1 if side == 0 else 0
-        along_x = pltpu.make_async_remote_copy(
-            src_ref=state.at[row], dst_ref=hx.at[k, side],
-            send_sem=hx_s.at[k, side], recv_sem=hx_r.at[k, side],
+        return pltpu.make_async_remote_copy(
+            src_ref=states[k].at[rows - 1 if side == 0 else 0, layer],
+            dst_ref=hx.at[k, side, layer],
+            send_sem=hx_s.at[k, side, layer], recv_sem=hx_r.at[k, side, layer],
             device_id=(lax.rem(t + step + tiles, tiles), d), device_id_type=MESH,
         )
-        along_l = pltpu.make_async_remote_copy(
-            src_ref=state.at[:, layer], dst_ref=hl.at[k, side],
+
+    def along_l(k, side):
+        step = 1 if side == 0 else -1
+        return pltpu.make_async_remote_copy(
+            src_ref=states[k].at[:, layers - 1 if side == 0 else 0],
+            dst_ref=hl.at[k, side],
             send_sem=hl_s.at[k, side], recv_sem=hl_r.at[k, side],
             device_id=(t, lax.rem(d + step + depths, depths)), device_id_type=MESH,
         )
-        return along_x, along_l
-
-    def sends(side):
-        if side == 0:
-            return t < tiles - 1, d < depths - 1
-        return t > 0, d > 0
-
-    def takes(side):
-        if side == 0:
-            return t > 0, d > 0
-        return t < tiles - 1, d < depths - 1
-
-    def halo_start(k):
+
+    send_x = (t < tiles - 1, t > 0)
+    send_l = (d < depths - 1, d > 0)
+    take_x = (t > 0, t < tiles - 1)
+    take_l = (d > 0, d < depths - 1)
+
+    def layer_start(k, layer):
         for side in range(2):
-            for copy, there in zip(halo(k, side), sends(side)):
-                pl.when(there)(copy.start)
-
-    def halo_wait(k):
+            pl.when(send_x[side])(along_x(k, side, layer).start)
+        if layer == layers - 1:
+            pl.when(send_l[0])(along_l(k, 0).start)
+        if layer == 0:
+            pl.when(send_l[1])(along_l(k, 1).start)
+
+    def layer_wait(k, layer):
+        if layer == 0:
+            pl.when(take_l[0])(along_l(k, 0).wait_recv)
+        if layer == layers - 1:
+            pl.when(take_l[1])(along_l(k, 1).wait_recv)
         for side in range(2):
-            for copy, there in zip(halo(k, side), takes(side)):
-                pl.when(there)(copy.wait_recv)
+            pl.when(take_x[side])(along_x(k, side, layer).wait_recv)
 
     def halo_sent(k):
         for side in range(2):
-            for copy, there in zip(halo(k, side), sends(side)):
-                pl.when(there)(copy.wait_send)
+            for layer in range(layers):
+                pl.when(send_x[side])(along_x(k, side, layer).wait_send)
+            pl.when(send_l[side])(along_l(k, side).wait_send)
 
     def top_copy(k, i):
         return pltpu.make_async_remote_copy(
@@ -192,30 +198,47 @@
     sub = iota((8, 8, 128), 1)
     plus = iota((8, 8, 128), 0) % ORB < 2
 
-    def stencil(k):
+    def stencil(k, l):
+        layer_wait(k, l)
         field, out = states[k], states[k + 1]
         for x in range(rows):
+            f = field[x, l]
+            beside = field[x, l - 1] if l > 0 else hl[k, 0, x]
+            beside += field[x, l + 1] if l < layers - 1 else hl[k, 1, x]
+            beside += field[x - 1, l] if x > 0 else hx[k, 0, l]
+            beside += field[x + 1, l] if x < rows - 1 else hx[k, 1, l]
+            r = pltpu.roll(f, 1, 2)
+            c = jnp.where(sub == 0, 0.0, pltpu.roll(r, 1, 1))
+            beside += jnp.where(lane == 0, c, r)
+            r = pltpu.roll(f, 127, 2)
+            c = jnp.where(sub == 7, 0.0, pltpu.roll(r, 7, 1))
+            beside += jnp.where(lane == 127, c, r)
+            onsite = (disorder[x, l] - CHEMICAL)[None] * f - HOPPING * beside
+            partner = jnp.concatenate([f[2:4], f[0:2], f[6:8], f[4:6]], axis=0)
+            new = jnp.where(plus, onsite, -onsite) + PAIRING * partner
+            if k > 0:
+                new = 2.0 * new - states[k - 1][x, l]
+            out[x, l] = new
+
+    def hand_out(state, out):
+        for x in range(rows):
             for l in range(layers):
-                f = field[x, l]
-                beside = field[x, l - 1] if l > 0 else hl[k, 0, x]
-                beside += field[x, l + 1] if l < layers - 1 else hl[k, 1, x]
-                beside += field[x - 1, l] if x > 0 else hx[k, 0, l]
-                beside += field[x + 1, l] if x < rows - 1 else hx[k, 1, l]
-                r = pltpu.roll(f, 1, 2)
-                c = jnp.where(sub == 0, 0.0, pltpu.roll(r, 1, 1))
-                beside += jnp.where(lane == 0, c, r)
-                r = pltpu.roll(f, 127, 2)
-                c = jnp.where(sub == 7, 0.0, pltpu.roll(r, 7, 1))
-                beside += jnp.where(lane == 127, c, r)
-                onsite = (disorder[x, l] - CHEMICAL)[None] * f - HOPPING * beside
-                partner = jnp.concatenate([f[2:4], f[0:2], f[6:8], f[4:6]], axis=0)
-                new = jnp.where(plus, onsite, -onsite) + PAIRING * partner
-                if k > 0:
-                    new = 2.0 * new - states[k - 1][x, l]
-                out[x, l] = new
-
-    halo_start(0)
+                for q in range(8):
+                    out[q % ORB, q // ORB, l, spread(x), :] = state[x, l, q]
+
+    for x in range(rows):
+        for l in order_l:
+            for q in range(8):
+                s0[x, l, q] = sub_in[q % ORB, q // ORB, l, spread(x), :]
+    pl.semaphore_wait(barrier, tiles - 1 + depths - 1)
+    for l in order_l:
+        layer_start(0, l)
     top_start(0)
+    for x in range(rows):
+        for l in range(layers):
+            disorder[x, l] = dis_in[l, spread(x), :]
+    for v in range(2):
+        adatoms[:, v * count : (v + 1) * count] = ad_in[:, v, :]
 
     b, c = block[...], coupling[...]
     cb = exact(c, b)
@@ -227,11 +250,11 @@
     pair2 = exact(cb, c, NT)
     values = exact(proj[...], adatoms[...])
     values = jnp.concatenate([values[:, :count], values[:, count:]], axis=0)
-    spot = spot_of[...]
+    spot = spot_of[...].reshape(1, count)
     row = iota(values.shape, 0)
     values = jnp.where(row == LIVE, 1.0, values)
-    values = jnp.where(row == HIGH, (spot // 128).astype(jnp.float32), values)
-    values = jnp.where(row == LOW, (spot % 128).astype(jnp.float32), values)
+    values = jnp.where(row == HIGH, (spot // 128 % 8).astype(jnp.float32), values)
+    values = jnp.where(row == LOW, (spot // 1024 * 128 + spot % 128).astype(jnp.float32), values)
     owner = (iota((tiles, count), 0) == tile_of[...]).astype(jnp.float32)
     earlier = (iota((count, count), 0) < iota((count, count), 1)).astype(jnp.float32)
     before = product(owner.astype(jnp.bfloat16), earlier.astype(jnp.bfloat16))
@@ -253,47 +276,43 @@
     each(tiles - 1, lambda i: go_copy(peer(i), t).start())
     got[t] = send[t]
 
-    halo_wait(0)
-    stencil(0)
+    for l in order_l:
+        stencil(0, l)
+        if l > 0:
+            layer_start(1, l)
+        else:
+            pl.when(d > 0)(lambda: layer_start(1, 0))
 
     each(tiles - 1, lambda i: go_copy(peer(i), peer(i)).wait_recv())
 
     order = [v * 16 + j * 4 + o for j in range(STEPS) for v in range(2) for o in range(ORB)]
     order.append(LIVE)
     terms = len(order)
+    wide = GROUP * slots
+
+    def group(g):
+        if tiles == GROUP:
+            return slice(0, wide)
+        return pl.ds(pl.multiple_of(g * wide, 128), wide)
 
     def scatter(g):
-        for i in range(GROUP):
-            u = g * GROUP + i
-            data = got[u]
-            first, second = halves(data)
-            here = iota((lines, slots), 0).astype(jnp.float32) == data[HIGH : HIGH + 1]
-            high[u] = here.astype(jnp.float32)
-            low = iota((128, slots), 0).astype(jnp.float32) == data[LOW : LOW + 1]
-            low_t[u] = low.astype(jnp.float32).astype(jnp.bfloat16)
-            for at, q in enumerate(order):
-                for p, part in enumerate((first, second)):
-                    if q == LIVE and p == 1:
-                        continue
-                    line = (p * terms + at) * lines
-                    lhs[line : line + lines, i * slots : (i + 1) * slots] = jnp.where(
-                        here, part[q : q + 1], 0.0
-                    ).astype(jnp.bfloat16)
-        total = jnp.zeros((lhs.shape[0], 128), jnp.float32)
-        for i in range(GROUP):
-            total += product(
-                lhs[:, i * slots : (i + 1) * slots], low_t[g * GROUP + i], NT
-            )
-        half = terms * lines
-        merged = total[: half - lines] + total[half:]
-        merged = merged.reshape(terms - 1, rows, 8, 128)
-        counted = total[half - lines : half].reshape(rows, 8, 128)
-        if tiles == GROUP:
-            scat[0 : terms - 1] = merged
-            scat[terms - 1] = counted
-        else:
-            scat[0 : terms - 1] += merged
-            scat[terms - 1] += counted
+        data = jnp.concatenate([got[g * GROUP + i] for i in range(GROUP)], axis=1)
+        first, second = halves(data)
+        here = iota((8, wide), 0).astype(jnp.float32) == data[HIGH : HIGH + 1]
+        high[:, group(g)] = here.astype(jnp.float32)
+        low = iota((sites, wide), 0).astype(jnp.float32) == data[LOW : LOW + 1]
+        low_t[:, group(g)] = low.astype(jnp.float32).astype(jnp.bfloat16)
+        for at, q in enumerate(order):
+            both = [jnp.where(here, part[q : q + 1], 0.0) for part in (first, second)]
+            lhs[at * 16 : at * 16 + 16] = jnp.concatenate(both, axis=0).astype(jnp.bfloat16)
+        total = product(lhs[...], low_t[:, group(g)], NT).reshape(terms, 2, 8, sites)
+        total = total[:, 0] + total[:, 1]
+        for x in range(rows):
+            part = total[:, :, x * 128 : x * 128 + 128]
+            if tiles == GROUP:
+                scat[:, x] = part
+            else:
+                scat[:, x] += part
 
     if tiles > GROUP:
         scat[...] = jnp.zeros_like(scat)
@@ -304,28 +323,19 @@
         partial_copy(0, d - 1).start()
         partial_copy(1, d - 1).start()
 
-    @pl.when(d == 0)
-    def _():
-        reduce_wait(0)
-        for x in range(rows):
-            s1[x, 0] += scat[0:8, x]
-
-    halo_start(1)
-    top_start(1)
-
     def gather(k):
         top_wait(k)
-        first, second = halves(top[k].reshape(rows * 8 * 8, 128))
-        both = jnp.concatenate([first, second], axis=0).astype(jnp.bfloat16)
-
-        def one(u):
-            found = product(both, low_t[u])
-            half = rows * 64
-            found = (found[:half] + found[half:]).reshape(rows, 8, 8, slots)
-            found = found * high[u].reshape(rows, 1, 8, slots)
-            ans[k, u] = jnp.sum(jnp.sum(found, axis=0), axis=1)
-
-        each(tiles, one)
+        field = jnp.concatenate([top[k, x].reshape(64, 128) for x in range(rows)], axis=1)
+        both = jnp.concatenate(halves(field), axis=0).astype(jnp.bfloat16)
+
+        def one(g):
+            found = product(both, low_t[:, group(g)])
+            found = (found[:64] + found[64:]).reshape(8, 8, wide) * high[:, group(g)][None]
+            found = jnp.sum(found, axis=1)
+            for i in range(GROUP):
+                ans[k, g * GROUP + i] = found[:, i * slots : (i + 1) * slots]
+
+        each(tiles // GROUP, one)
         each(tiles - 1, lambda i: answer_copy(k, peer(i), t).start())
         back[k, t] = ans[k, t]
 
@@ -355,8 +365,27 @@
         return jnp.concatenate(sums, axis=0)
 
     gather(0)
-    halo_wait(1)
-    stencil(1)
+
+    early = [l for l in order_l if l > 1]
+    for l in early:
+        stencil(1, l)
+        layer_start(2, l)
+
+    @pl.when(d == 0)
+    def _():
+        reduce_wait(0)
+        for x in range(rows):
+            s1[x, 0] += scat[0:8, x]
+        layer_start(1, 0)
+
+    top_start(1)
+
+    for l in order_l:
+        if l in early:
+            continue
+        stencil(1, l)
+        if l > 0:
+            layer_start(2, l)
 
     @pl.when(d == 0)
     def _():
@@ -365,13 +394,14 @@
             extra = scat[8:16, x] + scat[24, x][None] * mixed(pair1, s0, x)
             s2[x, 0] += 2.0 * extra
 
-    halo_start(2)
+    layer_start(2, 0)
     top_start(2)
     gather(1)
     a1[...] = adatom_part(0, adatoms[...])
     gather(2)
-    halo_wait(2)
-    stencil(2)
+    hand_out(s2, sub_prev)
+    for l in order_l:
+        stencil(2, l)
 
     @pl.when(d == 0)
     def _():
@@ -380,8 +410,15 @@
             extra = scat[16:24, x] + scat[24, x][None] * pairs
             s3[x, 0] += 2.0 * (2.0 * extra - scat[0:8, x])
 
+    hand_out(s3, sub_last)
+
+    def hand_adatoms(vectors, out):
+        for v in range(2):
+            out[:, v, :] = vectors[:, v * count : (v + 1) * count]
+
     a2[...] = 2.0 * adatom_part(1, a1[...]) - adatoms[...]
-    a3[...] = 2.0 * adatom_part(2, a2[...]) - a1[...]
+    hand_adatoms(a2[...], ad_prev)
+    hand_adatoms(2.0 * adatom_part(2, a2[...]) - a1[...], ad_last)
 
     each(tiles - 1, lambda i: go_copy(peer(i), t).wait_send())
     for k in range(STEPS):
@@ -408,14 +445,28 @@
     orba = adatom_block.shape[0]
     capacity = 2 * count // tiles
     slots = -(-capacity // 128) * 128
-    sites = substrate_start.reshape(orbs, vecs, layers, rows, 8, 128)
-    sites = sites.transpose(3, 2, 1, 0, 4, 5).reshape(rows, layers, 8, 8, 128)
-    potential = disorder.reshape(layers, rows, 8, 128).transpose(1, 0, 2, 3)
-    vectors = adatom_start.reshape(orba, vecs * count)
     f32 = jnp.float32
+
+    def lined(x):
+        lead = x.shape[:-2]
+        n = len(lead)
+        x = x.reshape(lead + (rows, 8, 128))
+        x = x.transpose(tuple(range(n)) + (n + 1, n, n + 2))
+        return x.reshape(lead + (8 * rows, 128))
+
+    def unlined(x):
+        lead = x.shape[:-2]
+        n = len(lead)
+        x = x.reshape(lead + (8, rows, 128))
+        x = x.transpose(tuple(range(n)) + (n + 1, n, n + 2))
+        return x.reshape(lead + (rows, cols))
+
+    sites = lined(substrate_start)
     state = jax.ShapeDtypeStruct(sites.shape, f32)
-    flat = jax.ShapeDtypeStruct(vectors.shape, f32)
-    lines = rows * 8
+    flat = jax.ShapeDtypeStruct(adatom_start.shape, f32)
+    block_state = pltpu.VMEM((rows, layers, 8, 8, 128), f32)
+    block_flat = pltpu.VMEM((orba, vecs * count), f32)
+    wide = GROUP * slots
     dma = pltpu.SemaphoreType.DMA
     vmem = pl.BlockSpec(memory_space=pltpu.VMEM)
     s2, s3, a2, a3 = pl.pallas_call(
@@ -424,15 +475,17 @@
         in_specs=[vmem] * 7,
         out_specs=(vmem,) * 4,
         scratch_shapes=[
-            pltpu.VMEM(sites.shape, f32),
+            block_state, block_state, block_state, block_state,
+            block_flat,
+            pltpu.VMEM((rows, layers, 8, 128), f32),
             pltpu.VMEM((STEPS, 2, layers, 8, 8, 128), f32),
             pltpu.VMEM((STEPS, 2, rows, 8, 8, 128), f32),
             pltpu.VMEM((STEPS, rows, 8, 8, 128), f32),
             pltpu.VMEM((tiles, 32, slots), f32),
             pltpu.VMEM((tiles, 32, slots), f32),
-            pltpu.VMEM((49 * lines, GROUP * slots), jnp.bfloat16),
-            pltpu.VMEM((tiles, 128, slots), jnp.bfloat16),
-            pltpu.VMEM((tiles, lines, slots), f32),
+            pltpu.VMEM((25 * 16, wide), jnp.bfloat16),
+            pltpu.VMEM((rows * 128, tiles * slots), jnp.bfloat16),
+            pltpu.VMEM((8, tiles * slots), f32),
             pltpu.VMEM((25, rows, 8, 128), f32),
             pltpu.VMEM((depths - 1, 8, rows, 8, 128), f32),
             pltpu.VMEM((depths - 1, 17, rows, 8, 128), f32),
@@ -440,8 +493,8 @@
             pltpu.VMEM((STEPS, tiles, 8, slots), f32),
             pltpu.VMEM((16, orba), f32),
             pltpu.VMEM((slots, count), jnp.bfloat16),
-            pltpu.VMEM(vectors.shape, f32),
-            dma((STEPS, 2)), dma((STEPS, 2)), dma((STEPS, 2)), dma((STEPS, 2)),
+            block_flat, block_flat,
+            dma((STEPS, 2, layers)), dma((STEPS, 2, layers)), dma((STEPS, 2)), dma((STEPS, 2)),
             dma((STEPS, depths - 1)), dma((STEPS,)),
             dma((tiles,)), dma((tiles,)),
             dma, dma((depths - 1,)), dma, dma((depths - 1,)),
@@ -451,15 +504,10 @@
             collective_id=0, has_side_effects=True, vmem_limit_bytes=56 * 1024 * 1024
         ),
     )(
-        sites, vectors, potential, adatom_block, coupling,
-        adatom_tile.reshape(1, count), adatom_spot.reshape(1, count),
+        sites, adatom_start, lined(disorder), adatom_block, coupling,
+        adatom_tile.reshape(1, count), adatom_spot,
     )
-
-    def unpack(s):
-        s = s.reshape(rows, layers, vecs, orbs, 8, 128).transpose(3, 2, 1, 0, 4, 5)
-        return s.reshape(substrate_start.shape)
-
-    return unpack(s2), unpack(s3), a2.reshape(adatom_start.shape), a3.reshape(adatom_start.shape)
+    return unlined(s2), unlined(s3), a2, a3
 
 
 def solution(mesh):

time: 50.3 us -> 42.7 us (0.85)
  the two profiles are of different devices: /device:TPU:0 before, /device:TPU:6 now
where the time goes in v2:
time: 42.7 us; the launch traced here: 42.4 us
  Pallas kernels  37.3 us (87%)
  local copies, waits for them, and re-layouts  4.48 us (10%)
  between operations  0.65 us (2%)
    pallas_call x1, Pallas kernels, per_device(): pl.pallas_call(functools.partial(kernel, tiles, depths), out_shape=(state...  37.3 us
    unnamed x10, local copies, waits for them, and re-layouts  4.48 us

profile of v2, /device:TPU:6, one launch (start us, length us, event | category | flops | bytes accessed | tf_op | source)
XLA Modules:
  0.0 42.4 jit_solution(1405693041988410641)
XLA Ops:
  0.6 37.3 %shard_map.102 = (f32[4,2,4,16,128]{4,3,2,1,0:T(8,128)}, f32[4,2,4,16,128]{4,3,2,1,0:T(8,128)}, f32[40,2,768]{2,1,0:T(2,128)}, f32[40,2,768]{2,1,0:T(2,128)}) custom-call(f32[4,2,4,16,128]{4,3,2,1,0:T(8,128)} %bitcast.21, f32[40,2,768]{2,1,0:T(2,128)} %ad_in.1, f32[4,16,128]{2,1,0:T(8,128)} %bitcast.24, f32[40,40]{1,0:T(8,128)} %block.1, f32[4,40]{1,0:T(4,128)} %coupling.1, ...), custom_call_target="tpu_custom_call" | custom-call | tf_op jit(solution)/shard_map/pallas_call | solution.py:472
  37.9 0.0 copy-start
  38.0 1.7 %copy.19 = f32[4,2,4,2,1024]{4,3,2,1,0:T(2,128)} copy(f32[4,2,4,2,1024]{4,3,2,1,0:T(2,128)} %bitcast.23) | data formatting | bytes 524288
  39.7 0.0 copy-done
  39.7 0.0 copy-start.2
  39.7 0.7 %copy.20 = f32[4,2,4,2,1024]{4,3,2,1,0:T(2,128)} copy(f32[4,2,4,2,1024]{4,3,2,1,0:T(2,128)S(1)} %bitcast.22) | data formatting | bytes 524288
  40.4 0.3 copy-done.2
  40.7 0.0 copy-start.1
  40.7 0.7 %copy.21 = f32[40,2,768]{2,1,0:T(2,128)} copy(f32[40,2,768]{2,1,0:T(2,128)S(1)} %copy-done.2) | data formatting | bytes 491520
  41.4 0.3 copy-done.1
  41.7 0.7 %copy.22 = f32[40,2,768]{2,1,0:T(2,128)} copy(f32[40,2,768]{2,1,0:T(2,128)S(1)} %copy-done.1) | data formatting | bytes 491520
Async XLA Ops:
  37.9 1.7 %copy-start = (f32[4,2,4,16,128]{4,3,2,1,0:T(8,128)S(1)}, f32[4,2,4,16,128]{4,3,2,1,0:T(8,128)}, u32[]{:S(2)}) copy-start(f32[4,2,4,16,128]{4,3,2,1,0:T(8,128)} %get-tuple-element.9) | copy-start | bytes 786436
  39.7 1.0 %copy-start.2 = (f32[40,2,768]{2,1,0:T(2,128)S(1)}, f32[40,2,768]{2,1,0:T(2,128)}, u32[]{:S(2)}) copy-start(f32[40,2,768]{2,1,0:T(2,128)} %get-tuple-element.18) | copy-start | bytes 737284
  40.7 1.0 %copy-start.1 = (f32[40,2,768]{2,1,0:T(2,128)S(1)}, f32[40,2,768]{2,1,0:T(2,128)}, u32[]{:S(2)}) copy-start(f32[40,2,768]{2,1,0:T(2,128)} %get-tuple-element.19) | copy-start | bytes 737284

commit v3 on v2

--- a/solution.py
+++ b/solution.py
@@ -230,6 +230,11 @@
         for l in order_l:
             for q in range(8):
                 s0[x, l, q] = sub_in[q % ORB, q // ORB, l, spread(x), :]
+    owner = (iota((tiles, count), 0) == tile_of[...]).astype(jnp.float32)
+    earlier = (iota((count, count), 0) < iota((count, count), 1)).astype(jnp.float32)
+    before = product(owner.astype(jnp.bfloat16), earlier.astype(jnp.bfloat16))
+    rank = jnp.sum(owner * before, axis=0, keepdims=True).astype(jnp.int32)
+    rank_t[...] = (iota((slots, count), 0) == rank).astype(jnp.float32).astype(jnp.bfloat16)
     pl.semaphore_wait(barrier, tiles - 1 + depths - 1)
     for l in order_l:
         layer_start(0, l)
@@ -255,11 +260,6 @@
     values = jnp.where(row == LIVE, 1.0, values)
     values = jnp.where(row == HIGH, (spot // 128 % 8).astype(jnp.float32), values)
     values = jnp.where(row == LOW, (spot // 1024 * 128 + spot % 128).astype(jnp.float32), values)
-    owner = (iota((tiles, count), 0) == tile_of[...]).astype(jnp.float32)
-    earlier = (iota((count, count), 0) < iota((count, count), 1)).astype(jnp.float32)
-    before = product(owner.astype(jnp.bfloat16), earlier.astype(jnp.bfloat16))
-    rank = jnp.sum(owner * before, axis=0, keepdims=True).astype(jnp.int32)
-    rank_t[...] = (iota((slots, count), 0) == rank).astype(jnp.float32).astype(jnp.bfloat16)
     parts = jnp.concatenate(halves(values), axis=0)
 
     def compact(g):
@@ -302,26 +302,29 @@
         high[:, group(g)] = here.astype(jnp.float32)
         low = iota((sites, wide), 0).astype(jnp.float32) == data[LOW : LOW + 1]
         low_t[:, group(g)] = low.astype(jnp.float32).astype(jnp.bfloat16)
-        for at, q in enumerate(order):
-            both = [jnp.where(here, part[q : q + 1], 0.0) for part in (first, second)]
-            lhs[at * 16 : at * 16 + 16] = jnp.concatenate(both, axis=0).astype(jnp.bfloat16)
-        total = product(lhs[...], low_t[:, group(g)], NT).reshape(terms, 2, 8, sites)
-        total = total[:, 0] + total[:, 1]
-        for x in range(rows):
-            part = total[:, :, x * 128 : x * 128 + 128]
+        for start, stop in ((0, 8), (8, terms)):
+            for at in range(start, stop):
+                q = order[at]
+                both = [jnp.where(here, part[q : q + 1], 0.0) for part in (first, second)]
+                lhs[at * 16 : at * 16 + 16] = jnp.concatenate(both, axis=0).astype(jnp.bfloat16)
+            total = product(lhs[start * 16 : stop * 16], low_t[:, group(g)], NT)
+            total = total.reshape(stop - start, 2, 8, sites)
+            total = total[:, 0] + total[:, 1]
+            for x in range(rows):
+                part = total[:, :, x * 128 : x * 128 + 128]
+                if tiles == GROUP:
+                    scat[start:stop, x] = part
+                else:
+                    scat[start:stop, x] += part
             if tiles == GROUP:
-                scat[:, x] = part
-            else:
-                scat[:, x] += part
+                pl.when(d > 0)(partial_copy(start // 8, d - 1).start)
 
     if tiles > GROUP:
         scat[...] = jnp.zeros_like(scat)
     each(tiles // GROUP, scatter)
-
-    @pl.when(d > 0)
-    def _():
-        partial_copy(0, d - 1).start()
-        partial_copy(1, d - 1).start()
+    if tiles > GROUP:
+        for part in range(2):
+            pl.when(d > 0)(partial_copy(part, d - 1).start)
 
     def gather(k):
         top_wait(k)
@@ -364,8 +367,6 @@
                 sums.append(total[None])
         return jnp.concatenate(sums, axis=0)
 
-    gather(0)
-
     early = [l for l in order_l if l > 1]
     for l in early:
         stencil(1, l)
@@ -379,6 +380,7 @@
         layer_start(1, 0)
 
     top_start(1)
+    gather(0)
 
     for l in order_l:
         if l in early:
@@ -397,7 +399,6 @@
     layer_start(2, 0)
     top_start(2)
     gather(1)
-    a1[...] = adatom_part(0, adatoms[...])
     gather(2)
     hand_out(s2, sub_prev)
     for l in order_l:
@@ -416,6 +417,7 @@
         for v in range(2):
             out[:, v, :] = vectors[:, v * count : (v + 1) * count]
 
+    a1[...] = adatom_part(0, adatoms[...])
     a2[...] = 2.0 * adatom_part(1, a1[...]) - adatoms[...]
     hand_adatoms(a2[...], ad_prev)
     hand_adatoms(2.0 * adatom_part(2, a2[...]) - a1[...], ad_last)
@@ -434,6 +436,36 @@
     def _():
         partial_copy(0, d - 1).wait_send()
         partial_copy(1, d - 1).wait_send()
+
+
+def settle(*arrays):
+    n = len(arrays)
+    chunks = 4
+
+    def body(*refs):
+        sems = refs[2 * n]
+        copies = []
+        for i in range(n):
+            step = refs[i].shape[0] // chunks
+            for j in range(chunks):
+                at = pl.ds(j * step, step)
+                copies.append(
+                    pltpu.make_async_copy(refs[i].at[at], refs[n + i].at[at], sems.at[i, j])
+                )
+        for copy in copies:
+            copy.start()
+        for copy in copies:
+            copy.wait()
+
+    anywhere = pl.BlockSpec(memory_space=pl.ANY)
+    return pl.pallas_call(
+        body,
+        out_shape=tuple(jax.ShapeDtypeStruct(x.shape, x.dtype) for x in arrays),
+        in_specs=[anywhere] * n,
+        out_specs=(anywhere,) * n,
+        scratch_shapes=[pltpu.SemaphoreType.DMA((n, chunks))],
+        compiler_params=pltpu.CompilerParams(vmem_limit_bytes=1 << 20),
+    )(*arrays)
 
 
 def per_device(
@@ -501,12 +533,13 @@
             dma((STEPS, tiles)), dma((STEPS, tiles)),
         ],
         compiler_params=pltpu.CompilerParams(
-            collective_id=0, has_side_effects=True, vmem_limit_bytes=56 * 1024 * 1024
+            collective_id=0, has_side_effects=True, vmem_limit_bytes=(56 if tiles > GROUP else 24) << 20
         ),
     )(
         sites, adatom_start, lined(disorder), adatom_block, coupling,
         adatom_tile.reshape(1, count), adatom_spot,
     )
+    s2, s3, a2, a3 = settle(s2, s3, a2, a3)
     return unlined(s2), unlined(s3), a2, a3
 
 

time: 42.7 us -> 42.5 us (level)
  the two profiles are of different devices: /device:TPU:6 before, /device:TPU:7 now
where the time goes in v3:
time: 42.5 us; the launch traced here: 42.1 us
  Pallas kernels  36 us (85%)
  local copies, waits for them, and re-layouts  5.42 us (13%)
  between operations  0.66 us (2%)
    pallas_call x1, Pallas kernels, per_device(): pl.pallas_call(functools.partial(kernel, tiles, depths), out_shape=(state...  35 us
    unnamed x14, local copies, waits for them, and re-layouts  5.42 us
    pallas_call x1, Pallas kernels, settle(): pl.pallas_call(body, out_shape=tuple((jax.ShapeDtypeStruct(x.shape, x.dty...  1.08 us

profile of v3, /device:TPU:7, one launch (start us, length us, event | category | flops | bytes accessed | tf_op | source)
XLA Modules:
  0.0 42.1 jit_solution(6742349850895630196)
XLA Ops:
  0.6 0.0 copy-start.4
  0.6 0.7 %copy-done.4 = s32[768]{0:T(1024)S(1)} copy-done((s32[768]{0:T(1024)S(1)}, s32[768]{0:T(1024)}, u32[]{:S(2)}) %copy-start.4) | copy-done | bytes 3096
  1.3 0.0 copy-start
  1.3 0.9 %copy-done = f32[4,2,4,2,1024]{4,3,2,1,0:T(2,128)S(1)} copy-done((f32[4,2,4,2,1024]{4,3,2,1,0:T(2,128)S(1)}, f32[4,2,4,2,1024]{4,3,2,1,0:T(2,128)}, u32[]{:S(2)}) %copy-start) | copy-done | bytes 262168
  2.3 0.0 copy-start.1
  2.3 0.9 %copy-done.1 = f32[40,2,768]{2,1,0:T(2,128)S(1)} copy-done((f32[40,2,768]{2,1,0:T(2,128)S(1)}, f32[40,2,768]{2,1,0:T(2,128)}, u32[]{:S(2)}) %copy-start.1) | copy-done | bytes 245784
  3.2 0.0 copy-start.2
  3.2 0.8 %copy-done.2 = f32[4,2,1024]{2,1,0:T(2,128)S(1)} copy-done((f32[4,2,1024]{2,1,0:T(2,128)S(1)}, f32[4,2,1024]{2,1,0:T(2,128)}, u32[]{:S(2)}) %copy-start.2) | copy-done | bytes 32792
  4.0 0.0 copy-start.3
  4.0 0.7 %copy-done.3 = f32[40,40]{1,0:T(8,128)S(1)} copy-done((f32[40,40]{1,0:T(8,128)S(1)}, f32[40,40]{1,0:T(8,128)}, u32[]{:S(2)}) %copy-start.3) | copy-done | bytes 6424
  4.7 0.0 copy-start.5
  4.7 0.7 %copy-done.5 = s32[768,1]{0,1:T(1,128)S(1)} copy-done((s32[768,1]{0,1:T(1,128)S(1)}, s32[768,1]{0,1:T(1,128)}, u32[]{:S(2)}) %copy-start.5) | copy-done | bytes 3096
  5.4 0.0 copy-start.6
  5.4 0.7 %copy-done.6 = f32[4,40]{1,0:T(4,128)S(1)} copy-done((f32[4,40]{1,0:T(4,128)S(1)}, f32[4,40]{1,0:T(4,128)}, u32[]{:S(2)}) %copy-start.6) | copy-done | bytes 664
  6.1 35.0 %shard_map.102 = (f32[4,2,4,16,128]{4,3,2,1,0:T(8,128)S(1)}, f32[4,2,4,16,128]{4,3,2,1,0:T(8,128)S(1)}, f32[40,2,768]{2,1,0:T(2,128)S(1)}, f32[40,2,768]{2,1,0:T(2,128)S(1)}) custom-call(f32[4,2,4,16,128]{4,3,2,1,0:T(8,128)S(1)} %bitcast.21, f32[40,2,768]{2,1,0:T(2,128)S(1)} %copy-done.1, f32[4,16,128]{2,1,0:T(8,128)S(1)} %bitcast.22, ...), custom_call_target="tpu_custom_call" | custom-call | tf_op jit(solution)/shard_map/pallas_call | solution.py:504
  41.0 1.1 %shard_map.103 = (f32[4,2,4,16,128]{4,3,2,1,0:T(8,128)}, f32[4,2,4,16,128]{4,3,2,1,0:T(8,128)}, f32[40,2,768]{2,1,0:T(2,128)}, f32[40,2,768]{2,1,0:T(2,128)}) custom-call(f32[4,2,4,16,128]{4,3,2,1,0:T(8,128)S(1)} %get-tuple-element.12.refs_0_, f32[4,2,4,16,128]{4,3,2,1,0:T(8,128)S(1)} %get-tuple-element.13.refs_1_, ...), custom_call_target="tpu_custom_call" | custom-call | tf_op jit(solution)/shard_map/pallas_call | solution.py:461
Async XLA Ops:
  0.6 0.7 %copy-start.4 = (s32[768]{0:T(1024)S(1)}, s32[768]{0:T(1024)}, u32[]{:S(2)}) copy-start(s32[768]{0:T(1024)} %spot_of.1) | copy-start | bytes 9220
  1.3 0.9 %copy-start = (f32[4,2,4,2,1024]{4,3,2,1,0:T(2,128)S(1)}, f32[4,2,4,2,1024]{4,3,2,1,0:T(2,128)}, u32[]{:S(2)}) copy-start(f32[4,2,4,2,1024]{4,3,2,1,0:T(2,128)} %param.7) | copy-start | bytes 786436
  2.3 0.9 %copy-start.1 = (f32[40,2,768]{2,1,0:T(2,128)S(1)}, f32[40,2,768]{2,1,0:T(2,128)}, u32[]{:S(2)}) copy-start(f32[40,2,768]{2,1,0:T(2,128)} %ad_in.1) | copy-start | bytes 737284
  3.2 0.8 %copy-start.2 = (f32[4,2,1024]{2,1,0:T(2,128)S(1)}, f32[4,2,1024]{2,1,0:T(2,128)}, u32[]{:S(2)}) copy-start(f32[4,2,1024]{2,1,0:T(2,128)} %param.9) | copy-start | bytes 98308
  4.0 0.7 %copy-start.3 = (f32[40,40]{1,0:T(8,128)S(1)}, f32[40,40]{1,0:T(8,128)}, u32[]{:S(2)}) copy-start(f32[40,40]{1,0:T(8,128)} %block.1) | copy-start | bytes 19204
  4.7 0.7 %copy-start.5 = (s32[768,1]{0,1:T(1,128)S(1)}, s32[768,1]{0,1:T(1,128)}, u32[]{:S(2)}) copy-start(s32[768,1]{0,1:T(1,128)} %param.12) | copy-start | bytes 9220
  5.4 0.7 %copy-start.6 = (f32[4,40]{1,0:T(4,128)S(1)}, f32[4,40]{1,0:T(4,128)}, u32[]{:S(2)}) copy-start(f32[4,40]{1,0:T(4,128)} %coupling.1) | copy-start | bytes 1924

commit v4 on v3

--- a/solution.py
+++ b/solution.py
@@ -13,7 +13,7 @@
 PAIRING = 0.3
 ORB = 4
 GROUP = 8
-LIVE, HIGH, LOW = 12, 13, 14
+HIGH, LOW = 8, 9
 
 MESH = pl.DeviceIdType.MESH
 HIGHEST = lax.Precision.HIGHEST
@@ -53,23 +53,37 @@
 
 def kernel(
     tiles, depths,
-    sub_in, ad_in, dis_in, block, coupling, tile_of, spot_of,
+    sub_hbm, ad_hbm, dis_hbm, block_hbm, coupling_hbm, tile_hbm, spot_hbm,
     sub_prev, sub_last, ad_prev, ad_last,
     s0, s1, s2, s3, adatoms, disorder,
     hx, hl, top, send, got, lhs, low_t, high, scat, red_a, red_b, ans, back, proj, rank_t, a1, a2,
+    sub_in, ad_in, dis_in, block, coupling, tile_of, spot_of, in_s,
     hx_s, hx_r, hl_s, hl_r, top_s, top_r, go_s, go_r, ra_s, ra_r, rb_s, rb_r, an_s, an_r,
 ):
     t = lax.axis_index("tile")
     d = lax.axis_index("depth")
     rows, layers = s0.shape[:2]
     count = tile_of.shape[1]
-    slots = send.shape[2]
+    capacity = 2 * count // tiles
+    slots = rank_t.shape[0]
+    packed = send.shape[2] == 24
+    each_wide = capacity if packed else slots
     sites = rows * 128
     states = [s0, s1, s2, s3]
     order_l = list(range(layers // 2, layers)) + list(range(layers // 2 - 1, -1, -1))
 
     def spread(x):
         return pl.ds(x, 8, stride=rows)
+
+    fetches = [
+        pltpu.make_async_copy(src, dst, in_s.at[i])
+        for i, (src, dst) in enumerate((
+            (tile_hbm, tile_of), (spot_hbm, spot_of), (coupling_hbm, coupling),
+            (ad_hbm, ad_in), (block_hbm, block), (sub_hbm, sub_in), (dis_hbm, dis_in),
+        ))
+    ]
+    for fetch in fetches:
+        fetch.start()
 
     barrier = pltpu.get_barrier_semaphore()
 
@@ -160,10 +174,10 @@
     def peer(i):
         return lax.rem(t + i + 1, tiles)
 
-    def go_copy(other, to):
+    def go_copy(part, other, to):
         return pltpu.make_async_remote_copy(
-            src_ref=send.at[other], dst_ref=got.at[to],
-            send_sem=go_s.at[other], recv_sem=go_r.at[to],
+            src_ref=send.at[part, other], dst_ref=got.at[part, to],
+            send_sem=go_s.at[part, other], recv_sem=go_r.at[part, to],
             device_id=(other, d), device_id_type=MESH,
         )
 
@@ -226,105 +240,149 @@
                 for q in range(8):
                     out[q % ORB, q // ORB, l, spread(x), :] = state[x, l, q]
 
-    for x in range(rows):
-        for l in order_l:
-            for q in range(8):
-                s0[x, l, q] = sub_in[q % ORB, q // ORB, l, spread(x), :]
+    half_lane = iota((8, 128), 1) < 64
+
+    def compact(part, values):
+        pieces = jnp.concatenate(halves(values), axis=0)
+
+        def one(g):
+            chosen = [
+                jnp.where(tile_of[...] == g * GROUP + i, pieces, 0.0).astype(jnp.bfloat16)
+                for i in range(GROUP)
+            ]
+            found = product(jnp.concatenate(chosen, axis=0), rank_t[...], NT)
+            for i in range(GROUP):
+                at = i * 32
+                mine = found[at : at + 16] + found[at + 16 : at + 32]
+                if packed:
+                    send[part, g * GROUP + i, 0:16] = mine[:, :128]
+                    tail = pltpu.roll(mine[8:16, 128:], 64, 1)
+                    send[part, g * GROUP + i, 16:24] = jnp.where(
+                        half_lane, mine[0:8, 128:], tail
+                    )
+                else:
+                    send[part, g * GROUP + i] = mine
+
+        each(tiles // GROUP, one)
+
+    def compact_start(part):
+        each(tiles - 1, lambda i: go_copy(part, peer(i), t).start())
+        got[part, t] = send[part, t]
+
+    fetches[0].wait()
     owner = (iota((tiles, count), 0) == tile_of[...]).astype(jnp.float32)
     earlier = (iota((count, count), 0) < iota((count, count), 1)).astype(jnp.float32)
     before = product(owner.astype(jnp.bfloat16), earlier.astype(jnp.bfloat16))
     rank = jnp.sum(owner * before, axis=0, keepdims=True).astype(jnp.int32)
     rank_t[...] = (iota((slots, count), 0) == rank).astype(jnp.float32).astype(jnp.bfloat16)
+
+    for fetch in fetches[1:4]:
+        fetch.wait()
+    for v in range(2):
+        adatoms[:, v * count : (v + 1) * count] = ad_in[:, v, :]
+    c = coupling[...]
+    values = exact(c, adatoms[...])
+    spot = spot_of[...].reshape(1, count)
+    row = iota((8, count), 0)
+    where = jnp.where(row == 0, (spot // 128 % 8 + 1).astype(jnp.float32), 0.0)
+    where = jnp.where(row == 1, (spot // 1024 * 128 + spot % 128).astype(jnp.float32), where)
+    compact(0, jnp.concatenate([values[:, :count], values[:, count:], where], axis=0))
+
+    for fetch in fetches[4:]:
+        fetch.wait()
+    for x in range(rows):
+        for l in order_l:
+            for q in range(8):
+                s0[x, l, q] = sub_in[q % ORB, q // ORB, l, spread(x), :]
     pl.semaphore_wait(barrier, tiles - 1 + depths - 1)
+    compact_start(0)
     for l in order_l:
         layer_start(0, l)
     top_start(0)
+
+    b = block[...]
+    cb = exact(c, b)
+    proj[0:4] = cb
+    proj[4:8] = exact(cb, b)
+    pair1 = exact(c, c, NT)
+    pair2 = exact(cb, c, NT)
+    values = exact(proj[...], adatoms[...])
+    compact(1, jnp.concatenate([values[:, :count], values[:, count:]], axis=0))
+    compact_start(1)
     for x in range(rows):
         for l in range(layers):
             disorder[x, l] = dis_in[l, spread(x), :]
-    for v in range(2):
-        adatoms[:, v * count : (v + 1) * count] = ad_in[:, v, :]
-
-    b, c = block[...], coupling[...]
-    cb = exact(c, b)
-    proj[0:4] = c
-    proj[4:8] = cb
-    proj[8:12] = exact(cb, b)
-    proj[12:16] = jnp.zeros((4, b.shape[0]), jnp.float32)
-    pair1 = exact(c, c, NT)
-    pair2 = exact(cb, c, NT)
-    values = exact(proj[...], adatoms[...])
-    values = jnp.concatenate([values[:, :count], values[:, count:]], axis=0)
-    spot = spot_of[...].reshape(1, count)
-    row = iota(values.shape, 0)
-    values = jnp.where(row == LIVE, 1.0, values)
-    values = jnp.where(row == HIGH, (spot // 128 % 8).astype(jnp.float32), values)
-    values = jnp.where(row == LOW, (spot // 1024 * 128 + spot % 128).astype(jnp.float32), values)
-    parts = jnp.concatenate(halves(values), axis=0)
-
-    def compact(g):
-        chosen = [
-            jnp.where(tile_of[...] == g * GROUP + i, parts, 0.0).astype(jnp.bfloat16)
-            for i in range(GROUP)
-        ]
-        packed = product(jnp.concatenate(chosen, axis=0), rank_t[...], NT)
-        for i in range(GROUP):
-            at = i * 64
-            send[g * GROUP + i] = packed[at : at + 32] + packed[at + 32 : at + 64]
-
-    each(tiles // GROUP, compact)
-    each(tiles - 1, lambda i: go_copy(peer(i), t).start())
-    got[t] = send[t]
-
+
+    wide = GROUP * each_wide
+
+    def group(g):
+        if tiles == GROUP:
+            return slice(0, wide)
+        return pl.ds(pl.multiple_of(g * wide, 128), wide)
+
+    def arrived(part, g):
+        blocks = [got[part, g * GROUP + i] for i in range(GROUP)]
+        if packed:
+            tails = []
+            for i in range(0, GROUP, 2):
+                one, two = blocks[i][16:24], blocks[i + 1][16:24]
+                upper = jnp.where(half_lane, one, pltpu.roll(two, 64, 1))
+                lower = jnp.where(half_lane, pltpu.roll(one, 64, 1), two)
+                tails.append(jnp.concatenate([upper, lower], axis=0))
+            blocks = [block_[0:16] for block_ in blocks] + tails
+        return jnp.concatenate(blocks, axis=1)
+
+    rows_b = [v * 8 + j * 4 + o for j in range(2) for v in range(2) for o in range(ORB)]
+
+    def scatter(part, g):
+        data = arrived(part, g)
+        if part == 0:
+            here = iota((8, wide), 0).astype(jnp.float32) + 1.0 == data[HIGH : HIGH + 1]
+            high[:, group(g)] = here.astype(jnp.float32)
+            low = iota((sites, wide), 0).astype(jnp.float32) == data[LOW : LOW + 1]
+            low_t[:, group(g)] = low.astype(jnp.float32).astype(jnp.bfloat16)
+        here = high[:, group(g)]
+        start, terms = (0, 8) if part == 0 else (8, 17)
+        first, second = halves(data)
+        for at, q in enumerate(range(8) if part == 0 else rows_b):
+            both = [here * piece[q : q + 1] for piece in (first, second)]
+            lhs[at * 16 : at * 16 + 16] = jnp.concatenate(both, axis=0).astype(jnp.bfloat16)
+        if part == 1:
+            both = jnp.concatenate([here, jnp.zeros_like(here)], axis=0)
+            lhs[256:272] = both.astype(jnp.bfloat16)
+        total = product(lhs[: terms * 16], low_t[:, group(g)], NT)
+        total = total.reshape(terms, 2, 8, sites)
+        total = total[:, 0] + total[:, 1]
+        for x in range(rows):
+            mine = total[:, :, x * 128 : x * 128 + 128]
+            if tiles == GROUP:
+                scat[start : start + terms, x] = mine
+            else:
+                scat[start : start + terms, x] += mine
+
+    if tiles > GROUP:
+        scat[...] = jnp.zeros_like(scat)
+
+    def scatter_all(part):
+        each(tiles - 1, lambda i: go_copy(part, peer(i), peer(i)).wait_recv())
+        each(tiles // GROUP, lambda g: scatter(part, g))
+        pl.when(d > 0)(partial_copy(part, d - 1).start)
+
+    scatter_all(0)
     for l in order_l:
         stencil(0, l)
         if l > 0:
             layer_start(1, l)
-        else:
-            pl.when(d > 0)(lambda: layer_start(1, 0))
-
-    each(tiles - 1, lambda i: go_copy(peer(i), peer(i)).wait_recv())
-
-    order = [v * 16 + j * 4 + o for j in range(STEPS) for v in range(2) for o in range(ORB)]
-    order.append(LIVE)
-    terms = len(order)
-    wide = GROUP * slots
-
-    def group(g):
-        if tiles == GROUP:
-            return slice(0, wide)
-        return pl.ds(pl.multiple_of(g * wide, 128), wide)
-
-    def scatter(g):
-        data = jnp.concatenate([got[g * GROUP + i] for i in range(GROUP)], axis=1)
-        first, second = halves(data)
-        here = iota((8, wide), 0).astype(jnp.float32) == data[HIGH : HIGH + 1]
-        high[:, group(g)] = here.astype(jnp.float32)
-        low = iota((sites, wide), 0).astype(jnp.float32) == data[LOW : LOW + 1]
-        low_t[:, group(g)] = low.astype(jnp.float32).astype(jnp.bfloat16)
-        for start, stop in ((0, 8), (8, terms)):
-            for at in range(start, stop):
-                q = order[at]
-                both = [jnp.where(here, part[q : q + 1], 0.0) for part in (first, second)]
-                lhs[at * 16 : at * 16 + 16] = jnp.concatenate(both, axis=0).astype(jnp.bfloat16)
-            total = product(lhs[start * 16 : stop * 16], low_t[:, group(g)], NT)
-            total = total.reshape(stop - start, 2, 8, sites)
-            total = total[:, 0] + total[:, 1]
-            for x in range(rows):
-                part = total[:, :, x * 128 : x * 128 + 128]
-                if tiles == GROUP:
-                    scat[start:stop, x] = part
-                else:
-                    scat[start:stop, x] += part
-            if tiles == GROUP:
-                pl.when(d > 0)(partial_copy(start // 8, d - 1).start)
-
-    if tiles > GROUP:
-        scat[...] = jnp.zeros_like(scat)
-    each(tiles // GROUP, scatter)
-    if tiles > GROUP:
-        for part in range(2):
-            pl.when(d > 0)(partial_copy(part, d - 1).start)
+
+    @pl.when(d == 0)
+    def _():
+        reduce_wait(0)
+        for x in range(rows):
+            s1[x, 0] += scat[0:8, x]
+
+    layer_start(1, 0)
+    top_start(1)
+    scatter_all(1)
 
     def gather(k):
         top_wait(k)
@@ -336,7 +394,13 @@
             found = (found[:64] + found[64:]).reshape(8, 8, wide) * high[:, group(g)][None]
             found = jnp.sum(found, axis=1)
             for i in range(GROUP):
-                ans[k, g * GROUP + i] = found[:, i * slots : (i + 1) * slots]
+                if packed:
+                    ans[k, g * GROUP + i, 0:8] = found[:, i * 128 : i * 128 + 128]
+                    at = (GROUP + i // 2) * 128
+                    tail = found[:, at : at + 128]
+                    ans[k, g * GROUP + i, 8:16] = tail if i % 2 == 0 else pltpu.roll(tail, 64, 1)
+                else:
+                    ans[k, g * GROUP + i] = found[:, i * slots : (i + 1) * slots]
 
         each(tiles // GROUP, one)
         each(tiles - 1, lambda i: answer_copy(k, peer(i), t).start())
@@ -344,7 +408,12 @@
 
     def below(k):
         each(tiles - 1, lambda i: answer_copy(k, peer(i), peer(i)).wait_recv())
-        first, second = halves(back[k].reshape(tiles * 8, slots))
+        if packed:
+            mine = [back[k, :, i : i + 8].reshape(tiles * 8, 128) for i in (0, 8)]
+            mine = jnp.concatenate(mine, axis=1)
+        else:
+            mine = back[k].reshape(tiles * 8, slots)
+        first, second = halves(mine)
         both = jnp.concatenate([first, second], axis=0).astype(jnp.bfloat16)
         found = product(both, rank_t[...])
         found = (found[: tiles * 8] + found[tiles * 8 :]).reshape(tiles, 8, count)
@@ -367,24 +436,8 @@
                 sums.append(total[None])
         return jnp.concatenate(sums, axis=0)
 
-    early = [l for l in order_l if l > 1]
-    for l in early:
-        stencil(1, l)
-        layer_start(2, l)
-
-    @pl.when(d == 0)
-    def _():
-        reduce_wait(0)
-        for x in range(rows):
-            s1[x, 0] += scat[0:8, x]
-        layer_start(1, 0)
-
-    top_start(1)
     gather(0)
-
     for l in order_l:
-        if l in early:
-            continue
         stencil(1, l)
         if l > 0:
             layer_start(2, l)
@@ -399,17 +452,23 @@
     layer_start(2, 0)
     top_start(2)
     gather(1)
+    hand_out(s2, sub_prev)
     gather(2)
-    hand_out(s2, sub_prev)
-    for l in order_l:
-        stencil(2, l)
 
     @pl.when(d == 0)
     def _():
         for x in range(rows):
             pairs = mixed(pair2, s0, x) + mixed(pair1, s1, x)
             extra = scat[16:24, x] + scat[24, x][None] * pairs
-            s3[x, 0] += 2.0 * (2.0 * extra - scat[0:8, x])
+            scat[16:24, x] = 2.0 * (2.0 * extra - scat[0:8, x])
+
+    for l in order_l:
+        stencil(2, l)
+
+    @pl.when(d == 0)
+    def _():
+        for x in range(rows):
+            s3[x, 0] += scat[16:24, x]
 
     hand_out(s3, sub_last)
 
@@ -422,7 +481,8 @@
     hand_adatoms(a2[...], ad_prev)
     hand_adatoms(2.0 * adatom_part(2, a2[...]) - a1[...], ad_last)
 
-    each(tiles - 1, lambda i: go_copy(peer(i), t).wait_send())
+    for part in range(2):
+        each(tiles - 1, lambda i: go_copy(part, peer(i), t).wait_send())
     for k in range(STEPS):
         halo_sent(k)
         each(tiles - 1, lambda i: answer_copy(k, peer(i), t).wait_send())
@@ -464,7 +524,7 @@
         in_specs=[anywhere] * n,
         out_specs=(anywhere,) * n,
         scratch_shapes=[pltpu.SemaphoreType.DMA((n, chunks))],
-        compiler_params=pltpu.CompilerParams(vmem_limit_bytes=1 << 20),
+        compiler_params=pltpu.CompilerParams(vmem_limit_bytes=56 << 20),
     )(*arrays)
 
 
@@ -498,13 +558,17 @@
     flat = jax.ShapeDtypeStruct(adatom_start.shape, f32)
     block_state = pltpu.VMEM((rows, layers, 8, 8, 128), f32)
     block_flat = pltpu.VMEM((orba, vecs * count), f32)
-    wide = GROUP * slots
+    packed = capacity == 192
+    each_wide = capacity if packed else slots
+    wide = GROUP * each_wide
+    sent = (24, 128) if packed else (16, slots)
+    answer = (16, 128) if packed else (8, slots)
     dma = pltpu.SemaphoreType.DMA
     vmem = pl.BlockSpec(memory_space=pltpu.VMEM)
     s2, s3, a2, a3 = pl.pallas_call(
         functools.partial(kernel, tiles, depths),
         out_shape=(state, state, flat, flat),
-        in_specs=[vmem] * 7,
+        in_specs=[pl.BlockSpec(memory_space=pltpu.HBM)] * 7,
         out_specs=(vmem,) * 4,
         scratch_shapes=[
             block_state, block_state, block_state, block_state,
@@ -513,27 +577,35 @@
             pltpu.VMEM((STEPS, 2, layers, 8, 8, 128), f32),
             pltpu.VMEM((STEPS, 2, rows, 8, 8, 128), f32),
             pltpu.VMEM((STEPS, rows, 8, 8, 128), f32),
-            pltpu.VMEM((tiles, 32, slots), f32),
-            pltpu.VMEM((tiles, 32, slots), f32),
-            pltpu.VMEM((25 * 16, wide), jnp.bfloat16),
-            pltpu.VMEM((rows * 128, tiles * slots), jnp.bfloat16),
-            pltpu.VMEM((8, tiles * slots), f32),
+            pltpu.VMEM((2, tiles) + sent, f32),
+            pltpu.VMEM((2, tiles) + sent, f32),
+            pltpu.VMEM((17 * 16, wide), jnp.bfloat16),
+            pltpu.VMEM((rows * 128, tiles * each_wide), jnp.bfloat16),
+            pltpu.VMEM((8, tiles * each_wide), f32),
             pltpu.VMEM((25, rows, 8, 128), f32),
             pltpu.VMEM((depths - 1, 8, rows, 8, 128), f32),
             pltpu.VMEM((depths - 1, 17, rows, 8, 128), f32),
-            pltpu.VMEM((STEPS, tiles, 8, slots), f32),
-            pltpu.VMEM((STEPS, tiles, 8, slots), f32),
-            pltpu.VMEM((16, orba), f32),
+            pltpu.VMEM((STEPS, tiles) + answer, f32),
+            pltpu.VMEM((STEPS, tiles) + answer, f32),
+            pltpu.VMEM((8, orba), f32),
             pltpu.VMEM((slots, count), jnp.bfloat16),
             block_flat, block_flat,
+            pltpu.VMEM(sites.shape, f32),
+            pltpu.VMEM(adatom_start.shape, f32),
+            pltpu.VMEM((layers, 8 * rows, 128), f32),
+            pltpu.VMEM(adatom_block.shape, f32),
+            pltpu.VMEM(coupling.shape, f32),
+            pltpu.VMEM((1, count), jnp.int32),
+            pltpu.VMEM((count,), jnp.int32),
+            dma((7,)),
             dma((STEPS, 2, layers)), dma((STEPS, 2, layers)), dma((STEPS, 2)), dma((STEPS, 2)),
             dma((STEPS, depths - 1)), dma((STEPS,)),
-            dma((tiles,)), dma((tiles,)),
+            dma((2, tiles)), dma((2, tiles)),
             dma, dma((depths - 1,)), dma, dma((depths - 1,)),
             dma((STEPS, tiles)), dma((STEPS, tiles)),
         ],
         compiler_params=pltpu.CompilerParams(
-            collective_id=0, has_side_effects=True, vmem_limit_bytes=(56 if tiles > GROUP else 24) << 20
+            collective_id=0, has_side_effects=True, vmem_limit_bytes=56 << 20
         ),
     )(
         sites, adatom_start, lined(disorder), adatom_block, coupling,

time: 42.5 us -> 65.7 us (1.55)
  the two profiles are of different devices: /device:TPU:7 before, /device:TPU:0 now
where the time goes in v4:
time: 65.7 us; the launch traced here: 65.2 us
  Pallas kernels  64.5 us (98%)
    pallas_call x1, Pallas kernels, per_device(): pl.pallas_call(functools.partial(kernel, tiles, depths), out_shape=(state...  32.5 us
    pallas_call x1, Pallas kernels, settle(): pl.pallas_call(body, out_shape=tuple((jax.ShapeDtypeStruct(x.shape, x.dty...  32 us

profile of v4, /device:TPU:0, one launch (start us, length us, event | category | flops | bytes accessed | tf_op | source)
XLA Modules:
  0.0 65.2 jit_solution(16953956883783668154)
XLA Ops:
  0.6 32.5 %shard_map.102 = (f32[4,2,4,16,128]{4,3,2,1,0:T(8,128)}, f32[4,2,4,16,128]{4,3,2,1,0:T(8,128)}, f32[40,2,768]{2,1,0:T(2,128)}, f32[40,2,768]{2,1,0:T(2,128)}) custom-call(f32[4,2,4,16,128]{4,3,2,1,0:T(8,128)} %bitcast.21, f32[40,2,768]{2,1,0:T(2,128)} %ad_hbm.1, f32[4,16,128]{2,1,0:T(8,128)} %bitcast.22, f32[40,40]{1,0:T(8,128)} %block_hbm.1, ...), custom_call_target="tpu_custom_call" | custom-call | tf_op jit(solution)/shard_map/pallas_call | solution.py:568
  33.2 32.0 %shard_map.103 = (f32[4,2,4,16,128]{4,3,2,1,0:T(8,128)}, f32[4,2,4,16,128]{4,3,2,1,0:T(8,128)}, f32[40,2,768]{2,1,0:T(2,128)}, f32[40,2,768]{2,1,0:T(2,128)}) custom-call(f32[4,2,4,16,128]{4,3,2,1,0:T(8,128)} %get-tuple-element.12.refs_0_, f32[4,2,4,16,128]{4,3,2,1,0:T(8,128)} %get-tuple-element.13.refs_1_, f32[40,2,768]{2,1,0:T(2,128)} %get-tuple-element.14.refs_2_, ...), custom_call_target="tpu_custom_call" | custom-call | tf_op jit(solution)/shard_map/pallas_call | solution.py:521

commit v5 on v4

--- a/solution.py
+++ b/solution.py
@@ -78,8 +78,8 @@
     fetches = [
         pltpu.make_async_copy(src, dst, in_s.at[i])
         for i, (src, dst) in enumerate((
-            (tile_hbm, tile_of), (spot_hbm, spot_of), (coupling_hbm, coupling),
-            (ad_hbm, ad_in), (block_hbm, block), (sub_hbm, sub_in), (dis_hbm, dis_in),
+            (sub_hbm, sub_in), (tile_hbm, tile_of), (spot_hbm, spot_of),
+            (coupling_hbm, coupling), (ad_hbm, ad_in), (dis_hbm, dis_in), (block_hbm, block),
         ))
     ]
     for fetch in fetches:
@@ -269,14 +269,25 @@
         each(tiles - 1, lambda i: go_copy(part, peer(i), t).start())
         got[part, t] = send[part, t]
 
-    fetches[0].wait()
+    for fetch in fetches[:1]:
+        fetch.wait()
+    for x in range(rows):
+        for l in order_l:
+            for q in range(8):
+                s0[x, l, q] = sub_in[q % ORB, q // ORB, l, spread(x), :]
+    pl.semaphore_wait(barrier, tiles - 1 + depths - 1)
+    for l in order_l:
+        layer_start(0, l)
+    top_start(0)
+
+    fetches[1].wait()
     owner = (iota((tiles, count), 0) == tile_of[...]).astype(jnp.float32)
     earlier = (iota((count, count), 0) < iota((count, count), 1)).astype(jnp.float32)
     before = product(owner.astype(jnp.bfloat16), earlier.astype(jnp.bfloat16))
     rank = jnp.sum(owner * before, axis=0, keepdims=True).astype(jnp.int32)
     rank_t[...] = (iota((slots, count), 0) == rank).astype(jnp.float32).astype(jnp.bfloat16)
 
-    for fetch in fetches[1:4]:
+    for fetch in fetches[2:5]:
         fetch.wait()
     for v in range(2):
         adatoms[:, v * count : (v + 1) * count] = ad_in[:, v, :]
@@ -287,28 +298,9 @@
     where = jnp.where(row == 0, (spot // 128 % 8 + 1).astype(jnp.float32), 0.0)
     where = jnp.where(row == 1, (spot // 1024 * 128 + spot % 128).astype(jnp.float32), where)
     compact(0, jnp.concatenate([values[:, :count], values[:, count:], where], axis=0))
-
-    for fetch in fetches[4:]:
+    compact_start(0)
+    for fetch in fetches[5:]:
         fetch.wait()
-    for x in range(rows):
-        for l in order_l:
-            for q in range(8):
-                s0[x, l, q] = sub_in[q % ORB, q // ORB, l, spread(x), :]
-    pl.semaphore_wait(barrier, tiles - 1 + depths - 1)
-    compact_start(0)
-    for l in order_l:
-        layer_start(0, l)
-    top_start(0)
-
-    b = block[...]
-    cb = exact(c, b)
-    proj[0:4] = cb
-    proj[4:8] = exact(cb, b)
-    pair1 = exact(c, c, NT)
-    pair2 = exact(cb, c, NT)
-    values = exact(proj[...], adatoms[...])
-    compact(1, jnp.concatenate([values[:, :count], values[:, count:]], axis=0))
-    compact_start(1)
     for x in range(rows):
         for l in range(layers):
             disorder[x, l] = dis_in[l, spread(x), :]
@@ -368,22 +360,6 @@
         each(tiles // GROUP, lambda g: scatter(part, g))
         pl.when(d > 0)(partial_copy(part, d - 1).start)
 
-    scatter_all(0)
-    for l in order_l:
-        stencil(0, l)
-        if l > 0:
-            layer_start(1, l)
-
-    @pl.when(d == 0)
-    def _():
-        reduce_wait(0)
-        for x in range(rows):
-            s1[x, 0] += scat[0:8, x]
-
-    layer_start(1, 0)
-    top_start(1)
-    scatter_all(1)
-
     def gather(k):
         top_wait(k)
         field = jnp.concatenate([top[k, x].reshape(64, 128) for x in range(rows)], axis=1)
@@ -420,10 +396,12 @@
         found = jnp.sum(found * owner.reshape(tiles, 1, count), axis=0)
         return jnp.concatenate([found[0:4], found[4:8]], axis=1)
 
-    ct = exact((iota(b.shape, 0) == iota(b.shape, 1)).astype(jnp.float32), c, NT)
-
     def adatom_part(k, vector):
         return exact(b, vector) + exact(ct, below(k))
+
+    def hand_adatoms(vectors, out):
+        for v in range(2):
+            out[:, v, :] = vectors[:, v * count : (v + 1) * count]
 
     def mixed(pair, state, x):
         sums = []
@@ -436,11 +414,43 @@
                 sums.append(total[None])
         return jnp.concatenate(sums, axis=0)
 
-    gather(0)
     for l in order_l:
+        if l == 0:
+            scatter_all(0)
+        stencil(0, l)
+        if l > 0:
+            layer_start(1, l)
+
+    @pl.when(d == 0)
+    def _():
+        reduce_wait(0)
+        for x in range(rows):
+            s1[x, 0] += scat[0:8, x]
+
+    layer_start(1, 0)
+    top_start(1)
+
+    b = block[...]
+    cb = exact(c, b)
+    proj[0:4] = cb
+    proj[4:8] = exact(cb, b)
+    pair1 = exact(c, c, NT)
+    pair2 = exact(cb, c, NT)
+    ct = exact((iota(b.shape, 0) == iota(b.shape, 1)).astype(jnp.float32), c, NT)
+    values = exact(proj[...], adatoms[...])
+    compact(1, jnp.concatenate([values[:, :count], values[:, count:]], axis=0))
+    compact_start(1)
+
+    between = [lambda: gather(0), lambda: gather(1), lambda: scatter_all(1)]
+    for l in order_l:
+        if l == 0:
+            for work in between:
+                work()
         stencil(1, l)
         if l > 0:
             layer_start(2, l)
+            if between:
+                between.pop(0)()
 
     @pl.when(d == 0)
     def _():
@@ -451,8 +461,8 @@
 
     layer_start(2, 0)
     top_start(2)
-    gather(1)
     hand_out(s2, sub_prev)
+    a1[...] = adatom_part(0, adatoms[...])
     gather(2)
 
     @pl.when(d == 0)
@@ -462,6 +472,8 @@
             extra = scat[16:24, x] + scat[24, x][None] * pairs
             scat[16:24, x] = 2.0 * (2.0 * extra - scat[0:8, x])
 
+    a2[...] = 2.0 * adatom_part(1, a1[...]) - adatoms[...]
+    hand_adatoms(a2[...], ad_prev)
     for l in order_l:
         stencil(2, l)
 
@@ -472,13 +484,6 @@
 
     hand_out(s3, sub_last)
 
-    def hand_adatoms(vectors, out):
-        for v in range(2):
-            out[:, v, :] = vectors[:, v * count : (v + 1) * count]
-
-    a1[...] = adatom_part(0, adatoms[...])
-    a2[...] = 2.0 * adatom_part(1, a1[...]) - adatoms[...]
-    hand_adatoms(a2[...], ad_prev)
     hand_adatoms(2.0 * adatom_part(2, a2[...]) - a1[...], ad_last)
 
     for part in range(2):
@@ -500,22 +505,28 @@
 
 def settle(*arrays):
     n = len(arrays)
-    chunks = 4
+    chunks = 2
 
     def body(*refs):
-        sems = refs[2 * n]
-        copies = []
+        held, sems = refs[2 * n : 3 * n], refs[3 * n]
+        copies, leaves = [], []
         for i in range(n):
             step = refs[i].shape[0] // chunks
             for j in range(chunks):
                 at = pl.ds(j * step, step)
                 copies.append(
-                    pltpu.make_async_copy(refs[i].at[at], refs[n + i].at[at], sems.at[i, j])
+                    pltpu.make_async_copy(refs[i].at[at], held[i].at[at], sems.at[0, i, j])
+                )
+                leaves.append(
+                    pltpu.make_async_copy(held[i].at[at], refs[n + i].at[at], sems.at[1, i, j])
                 )
         for copy in copies:
             copy.start()
-        for copy in copies:
+        for copy, leave in zip(copies, leaves):
             copy.wait()
+            leave.start()
+        for leave in leaves:
+            leave.wait()
 
     anywhere = pl.BlockSpec(memory_space=pl.ANY)
     return pl.pallas_call(
@@ -523,7 +534,8 @@
         out_shape=tuple(jax.ShapeDtypeStruct(x.shape, x.dtype) for x in arrays),
         in_specs=[anywhere] * n,
         out_specs=(anywhere,) * n,
-        scratch_shapes=[pltpu.SemaphoreType.DMA((n, chunks))],
+        scratch_shapes=[pltpu.VMEM(x.shape, x.dtype) for x in arrays]
+        + [pltpu.SemaphoreType.DMA((2, n, chunks))],
         compiler_params=pltpu.CompilerParams(vmem_limit_bytes=56 << 20),
     )(*arrays)
 

time: 65.7 us -> 43 us (0.65)
  Pallas kernels: 64.5 us -> 41.5 us
    pallas_call x1, Pallas kernels: 32 us -> 2.07 us  [settle(): pl.pallas_call(body, out_shape=tuple((jax.ShapeDtypeStruct(x.shape, x.dty...]
    pallas_call x1, Pallas kernels: 32.5 us -> 39.4 us  [per_device(): pl.pallas_call(functools.partial(kernel, tiles, depths), out_shape=(state...]
where the time goes in v5:
time: 43 us; the launch traced here: 42.1 us
  Pallas kernels  41.5 us (97%)
  between operations  0.64 us (1%)
    pallas_call x1, Pallas kernels, per_device(): pl.pallas_call(functools.partial(kernel, tiles, depths), out_shape=(state...  39.4 us
    pallas_call x1, Pallas kernels, settle(): pl.pallas_call(body, out_shape=tuple((jax.ShapeDtypeStruct(x.shape, x.dty...  2.07 us

profile of v5, /device:TPU:0, one launch (start us, length us, event | category | flops | bytes accessed | tf_op | source)
XLA Modules:
  0.0 42.1 jit_solution(6352985972893955699)
XLA Ops:
  0.6 39.4 %shard_map.102 = (f32[4,2,4,16,128]{4,3,2,1,0:T(8,128)}, f32[4,2,4,16,128]{4,3,2,1,0:T(8,128)}, f32[40,2,768]{2,1,0:T(2,128)}, f32[40,2,768]{2,1,0:T(2,128)}) custom-call(f32[4,2,4,16,128]{4,3,2,1,0:T(8,128)} %bitcast.21, f32[40,2,768]{2,1,0:T(2,128)} %ad_hbm.1, f32[4,16,128]{2,1,0:T(8,128)} %bitcast.22, f32[40,40]{1,0:T(8,128)} %block_hbm.1, ...), custom_call_target="tpu_custom_call" | custom-call | tf_op jit(solution)/shard_map/pallas_call | solution.py:580
  40.1 2.1 %shard_map.103 = (f32[4,2,4,16,128]{4,3,2,1,0:T(8,128)}, f32[4,2,4,16,128]{4,3,2,1,0:T(8,128)}, f32[40,2,768]{2,1,0:T(2,128)}, f32[40,2,768]{2,1,0:T(2,128)}) custom-call(f32[4,2,4,16,128]{4,3,2,1,0:T(8,128)} %get-tuple-element.12.refs_0_, f32[4,2,4,16,128]{4,3,2,1,0:T(8,128)} %get-tuple-element.13.refs_1_, f32[40,2,768]{2,1,0:T(2,128)} %get-tuple-element.14.refs_2_, ...), custom_call_target="tpu_custom_call" | custom-call | tf_op jit(solution)/shard_map/pallas_call | solution.py:532

commit v6 on v5

--- a/solution.py
+++ b/solution.py
@@ -78,7 +78,7 @@
     fetches = [
         pltpu.make_async_copy(src, dst, in_s.at[i])
         for i, (src, dst) in enumerate((
-            (sub_hbm, sub_in), (tile_hbm, tile_of), (spot_hbm, spot_of),
+            (tile_hbm, tile_of), (sub_hbm, sub_in), (spot_hbm, spot_of),
             (coupling_hbm, coupling), (ad_hbm, ad_in), (dis_hbm, dis_in), (block_hbm, block),
         ))
     ]
@@ -269,23 +269,22 @@
         each(tiles - 1, lambda i: go_copy(part, peer(i), t).start())
         got[part, t] = send[part, t]
 
-    for fetch in fetches[:1]:
-        fetch.wait()
+    fetches[0].wait()
+    owner = (iota((tiles, count), 0) == tile_of[...]).astype(jnp.float32)
+    earlier = (iota((count, count), 0) < iota((count, count), 1)).astype(jnp.float32)
+    before = product(owner.astype(jnp.bfloat16), earlier.astype(jnp.bfloat16))
+    rank = jnp.sum(owner * before, axis=0, keepdims=True).astype(jnp.int32)
+    rank_t[...] = (iota((slots, count), 0) == rank).astype(jnp.float32).astype(jnp.bfloat16)
+
+    fetches[1].wait()
     for x in range(rows):
         for l in order_l:
             for q in range(8):
                 s0[x, l, q] = sub_in[q % ORB, q // ORB, l, spread(x), :]
     pl.semaphore_wait(barrier, tiles - 1 + depths - 1)
-    for l in order_l:
+    for l in order_l[: layers // 2]:
         layer_start(0, l)
-    top_start(0)
-
-    fetches[1].wait()
-    owner = (iota((tiles, count), 0) == tile_of[...]).astype(jnp.float32)
-    earlier = (iota((count, count), 0) < iota((count, count), 1)).astype(jnp.float32)
-    before = product(owner.astype(jnp.bfloat16), earlier.astype(jnp.bfloat16))
-    rank = jnp.sum(owner * before, axis=0, keepdims=True).astype(jnp.int32)
-    rank_t[...] = (iota((slots, count), 0) == rank).astype(jnp.float32).astype(jnp.bfloat16)
+
 
     for fetch in fetches[2:5]:
         fetch.wait()
@@ -299,6 +298,9 @@
     where = jnp.where(row == 1, (spot // 1024 * 128 + spot % 128).astype(jnp.float32), where)
     compact(0, jnp.concatenate([values[:, :count], values[:, count:], where], axis=0))
     compact_start(0)
+    for l in order_l[layers // 2 :]:
+        layer_start(0, l)
+    top_start(0)
     for fetch in fetches[5:]:
         fetch.wait()
     for x in range(rows):
@@ -414,22 +416,6 @@
                 sums.append(total[None])
         return jnp.concatenate(sums, axis=0)
 
-    for l in order_l:
-        if l == 0:
-            scatter_all(0)
-        stencil(0, l)
-        if l > 0:
-            layer_start(1, l)
-
-    @pl.when(d == 0)
-    def _():
-        reduce_wait(0)
-        for x in range(rows):
-            s1[x, 0] += scat[0:8, x]
-
-    layer_start(1, 0)
-    top_start(1)
-
     b = block[...]
     cb = exact(c, b)
     proj[0:4] = cb
@@ -441,16 +427,28 @@
     compact(1, jnp.concatenate([values[:, :count], values[:, count:]], axis=0))
     compact_start(1)
 
-    between = [lambda: gather(0), lambda: gather(1), lambda: scatter_all(1)]
+    scatter_all(0)
     for l in order_l:
-        if l == 0:
-            for work in between:
-                work()
+        stencil(0, l)
+        if l > 0:
+            layer_start(1, l)
+
+    @pl.when(d == 0)
+    def _():
+        reduce_wait(0)
+        for x in range(rows):
+            s1[x, 0] += scat[0:8, x]
+
+    top_start(1)
+    layer_start(1, 0)
+
+    scatter_all(1)
+    gather(0)
+    gather(1)
+    for l in order_l:
         stencil(1, l)
         if l > 0:
             layer_start(2, l)
-            if between:
-                between.pop(0)()
 
     @pl.when(d == 0)
     def _():
@@ -459,8 +457,8 @@
             extra = scat[8:16, x] + scat[24, x][None] * mixed(pair1, s0, x)
             s2[x, 0] += 2.0 * extra
 
+    top_start(2)
     layer_start(2, 0)
-    top_start(2)
     hand_out(s2, sub_prev)
     a1[...] = adatom_part(0, adatoms[...])
     gather(2)

time: 43 us -> 36.5 us (0.85); the launches traced: 42.1 us -> 36.3 us
  Pallas kernels: 41.5 us -> 35.6 us
    pallas_call x1, Pallas kernels: 39.4 us -> 33.6 us  [per_device(): pl.pallas_call(functools.partial(kernel, tiles, depths), out_shape=(state...]
where the time goes in v6:
time: 36.5 us; the launch traced here: 36.3 us
  Pallas kernels  35.6 us (98%)
  between operations  0.64 us (2%)
    pallas_call x1, Pallas kernels, per_device(): pl.pallas_call(functools.partial(kernel, tiles, depths), out_shape=(state...  33.6 us
    pallas_call x1, Pallas kernels, settle(): pl.pallas_call(body, out_shape=tuple((jax.ShapeDtypeStruct(x.shape, x.dty...  2.07 us

profile of v6, /device:TPU:0, one launch (start us, length us, event | category | flops | bytes accessed | tf_op | source)
XLA Modules:
  0.0 36.3 jit_solution(11002586461943635100)
XLA Ops:
  0.6 33.6 %shard_map.102 = (f32[4,2,4,16,128]{4,3,2,1,0:T(8,128)}, f32[4,2,4,16,128]{4,3,2,1,0:T(8,128)}, f32[40,2,768]{2,1,0:T(2,128)}, f32[40,2,768]{2,1,0:T(2,128)}) custom-call(f32[4,2,4,16,128]{4,3,2,1,0:T(8,128)} %bitcast.21, f32[40,2,768]{2,1,0:T(2,128)} %ad_hbm.1, f32[4,16,128]{2,1,0:T(8,128)} %bitcast.22, f32[40,40]{1,0:T(8,128)} %block_hbm.1, ...), custom_call_target="tpu_custom_call" | custom-call | tf_op jit(solution)/shard_map/pallas_call | solution.py:578
  34.2 2.1 %shard_map.103 = (f32[4,2,4,16,128]{4,3,2,1,0:T(8,128)}, f32[4,2,4,16,128]{4,3,2,1,0:T(8,128)}, f32[40,2,768]{2,1,0:T(2,128)}, f32[40,2,768]{2,1,0:T(2,128)}) custom-call(f32[4,2,4,16,128]{4,3,2,1,0:T(8,128)} %get-tuple-element.12.refs_0_, f32[4,2,4,16,128]{4,3,2,1,0:T(8,128)} %get-tuple-element.13.refs_1_, f32[40,2,768]{2,1,0:T(2,128)} %get-tuple-element.14.refs_2_, ...), custom_call_target="tpu_custom_call" | custom-call | tf_op jit(solution)/shard_map/pallas_call | solution.py:530

commit v7 on v6

--- a/solution.py
+++ b/solution.py
@@ -70,7 +70,7 @@
     each_wide = capacity if packed else slots
     sites = rows * 128
     states = [s0, s1, s2, s3]
-    order_l = list(range(layers // 2, layers)) + list(range(layers // 2 - 1, -1, -1))
+    order_l = [1, 0] + list(range(2, layers)) if layers > 1 else [0]
 
     def spread(x):
         return pl.ds(x, 8, stride=rows)
@@ -428,37 +428,40 @@
     compact_start(1)
 
     scatter_all(0)
+    def add_first():
+        reduce_wait(0)
+        for x in range(rows):
+            s1[x, 0] += scat[0:8, x]
+
+    def add_second():
+        for x in range(rows):
+            s2[x, 0] += scat[8:16, x]
+
     for l in order_l:
         stencil(0, l)
-        if l > 0:
-            layer_start(1, l)
-
-    @pl.when(d == 0)
-    def _():
-        reduce_wait(0)
-        for x in range(rows):
-            s1[x, 0] += scat[0:8, x]
-
-    top_start(1)
-    layer_start(1, 0)
+        if l == 0:
+            pl.when(d == 0)(add_first)
+            top_start(1)
+        layer_start(1, l)
 
     scatter_all(1)
     gather(0)
     gather(1)
-    for l in order_l:
-        stencil(1, l)
-        if l > 0:
-            layer_start(2, l)
 
     @pl.when(d == 0)
     def _():
         reduce_wait(1)
         for x in range(rows):
             extra = scat[8:16, x] + scat[24, x][None] * mixed(pair1, s0, x)
-            s2[x, 0] += 2.0 * extra
-
-    top_start(2)
-    layer_start(2, 0)
+            scat[8:16, x] = 2.0 * extra
+
+    for l in order_l:
+        stencil(1, l)
+        if l == 0:
+            pl.when(d == 0)(add_second)
+            top_start(2)
+        layer_start(2, l)
+
     hand_out(s2, sub_prev)
     a1[...] = adatom_part(0, adatoms[...])
     gather(2)

time: 36.5 us -> 37.7 us (1.033)
  Pallas kernels: 35.6 us -> 36.9 us
    pallas_call x1, Pallas kernels: 33.6 us -> 34.8 us  [per_device(): pl.pallas_call(functools.partial(kernel, tiles, depths), out_shape=(state...]
where the time goes in v7:
time: 37.7 us; the launch traced here: 37.5 us
  Pallas kernels  36.9 us (98%)
  between operations  0.64 us (2%)
    pallas_call x1, Pallas kernels, per_device(): pl.pallas_call(functools.partial(kernel, tiles, depths), out_shape=(state...  34.8 us
    pallas_call x1, Pallas kernels, settle(): pl.pallas_call(body, out_shape=tuple((jax.ShapeDtypeStruct(x.shape, x.dty...  2.07 us

profile of v7, /device:TPU:0, one launch (start us, length us, event | category | flops | bytes accessed | tf_op | source)
XLA Modules:
  0.0 37.5 jit_solution(1088144508743758985)
XLA Ops:
  0.6 34.8 %shard_map.102 = (f32[4,2,4,16,128]{4,3,2,1,0:T(8,128)}, f32[4,2,4,16,128]{4,3,2,1,0:T(8,128)}, f32[40,2,768]{2,1,0:T(2,128)}, f32[40,2,768]{2,1,0:T(2,128)}) custom-call(f32[4,2,4,16,128]{4,3,2,1,0:T(8,128)} %bitcast.21, f32[40,2,768]{2,1,0:T(2,128)} %ad_hbm.1, f32[4,16,128]{2,1,0:T(8,128)} %bitcast.22, f32[40,40]{1,0:T(8,128)} %block_hbm.1, ...), custom_call_target="tpu_custom_call" | custom-call | tf_op jit(solution)/shard_map/pallas_call | solution.py:581
  35.5 2.1 %shard_map.103 = (f32[4,2,4,16,128]{4,3,2,1,0:T(8,128)}, f32[4,2,4,16,128]{4,3,2,1,0:T(8,128)}, f32[40,2,768]{2,1,0:T(2,128)}, f32[40,2,768]{2,1,0:T(2,128)}) custom-call(f32[4,2,4,16,128]{4,3,2,1,0:T(8,128)} %get-tuple-element.12.refs_0_, f32[4,2,4,16,128]{4,3,2,1,0:T(8,128)} %get-tuple-element.13.refs_1_, f32[40,2,768]{2,1,0:T(2,128)} %get-tuple-element.14.refs_2_, ...), custom_call_target="tpu_custom_call" | custom-call | tf_op jit(solution)/shard_map/pallas_call | solution.py:533
